TPU v7x, 32 devices: a whole 2x2x4 slice. The times are simulated.
32 devices in a mesh: seq: 4 (over y, x), inner: 8 (over z, core).
Axes of the slice: x: 2, y: 2, z: 4, core: 2. Of those that a mesh axis runs over, the one named last changes fastest.
Arguments:
- queries: bfloat16 [4096, 1024], P('seq', 'inner'), may hold values from -6 to 6
- key_vectors: bfloat16 [4096, 1024], P('seq', 'inner'), may hold values from -6 to 6
- value_vectors: bfloat16 [4096, 1024], P('seq', 'inner'), may hold values from -6 to 6
- out_grad: bfloat16 [4096, 1024], P('seq', 'inner'), may hold values from -6 to 6
Outputs:
- attended: bfloat16 [4096, 1024], P('seq', 'inner')
- query_grad: bfloat16 [4096, 1024], P('seq', 'inner')
- key_grad: bfloat16 [4096, 1024], P('seq', 'inner')
- value_grad: bfloat16 [4096, 1024], P('seq', 'inner')
All inputs are finite; a program needn't handle non-finite values.
Results may differ from a plain program's by a relative error of at most 0.0058.
Values sent between devices are 32-bit elements; how exact they have to be, the bound alone decides.
A program may use at most 64 MiB of HBM per device.

v0:
```python
import jax
import jax.numpy as jnp
from jax import lax
from jax.sharding import PartitionSpec as P

BLOCK = 512


def from_partner(value, axis, bit):
    mask = 2**bit
    pairs = [(source, source ^ mask) for source in range(lax.axis_size(axis))]
    return lax.ppermute(value, axis, pairs)


def prefix(part, axis, combine, identity, reverse):
    count = lax.axis_size(axis)
    place = lax.axis_index(axis)
    ahead = count - 1 - place if reverse else place
    gathered = lax.all_gather(part, axis)
    state = jnp.zeros_like(part) + jnp.asarray(identity, part.dtype)

    def one(step, state):
        source = count - 1 - step if reverse else step
        return combine(state, lax.dynamic_index_in_dim(gathered, source, 0, False))

    return lax.fori_loop(0, ahead, one, state)


def add_states(earlier, later):
    return jax.tree.map(jnp.add, earlier, later)


def per_device(queries, key_vectors, value_vectors, out_grad):
    half_rows, width = queries.shape
    count = half_rows // BLOCK
    side = lax.axis_index("inner") % 2
    is_second = side == 1
    position = (
        lax.axis_index("seq") * 2 * half_rows + side * half_rows + jnp.arange(half_rows)
    ).astype(jnp.float32)
    scaling = 1.0 / jnp.sqrt(width * (position + 1.0))
    scaled_grad = (scaling[:, None] * out_grad.astype(jnp.float32)).astype(jnp.bfloat16)
    scale_blocks = scaling.reshape(count, BLOCK)
    query_b = queries.reshape(count, BLOCK, width)
    key_b = key_vectors.reshape(count, BLOCK, width)
    value_b = value_vectors.reshape(count, BLOCK, width)
    grad_b = scaled_grad.reshape(count, BLOCK, width)
    outer_kv = jnp.einsum("nbd,nbv->ndv", key_b, value_b, preferred_element_type=jnp.float32)
    outer_back = jnp.einsum("nbd,nbv->ndv", query_b, grad_b, preferred_element_type=jnp.float32)
    local_kv = jnp.sum(outer_kv, 0)
    local_back = jnp.sum(outer_back, 0)
    zero_state = jnp.zeros_like(local_kv)
    other_kv, other_back = from_partner((local_kv, local_back), "inner", 0)
    earlier = prefix(local_kv + other_kv, "seq", add_states, zero_state, False)
    later = prefix(local_back + other_back, "seq", add_states, zero_state, True)
    state_in = earlier + jnp.where(is_second, other_kv, 0.0)
    back_in = later + jnp.where(is_second, 0.0, other_back)
    kv_used = (state_in[None] + jnp.cumsum(outer_kv, 0) - outer_kv).astype(jnp.bfloat16)
    back_used = (back_in[None] + (local_back[None] - jnp.cumsum(outer_back, 0))).astype(
        jnp.bfloat16
    )
    row_ids = jnp.arange(BLOCK)
    causal = (row_ids[:, None] >= row_ids[None, :])[None]
    scores = jnp.einsum("nbd,ncd->nbc", query_b, key_b, preferred_element_type=jnp.float32)
    weights = jnp.where(causal, scores, 0.0).astype(jnp.bfloat16)
    local = jnp.einsum("nbc,ncv->nbv", weights, value_b, preferred_element_type=jnp.float32)
    carried = jnp.einsum("nbd,ndv->nbv", query_b, kv_used, preferred_element_type=jnp.float32)
    attended = ((local + carried) * scale_blocks[..., None]).astype(jnp.bfloat16)
    grad_scores = jnp.where(
        causal, jnp.einsum("nbv,ncv->nbc", grad_b, value_b, preferred_element_type=jnp.float32), 0.0
    ).astype(jnp.bfloat16)
    query_grad = jnp.einsum(
        "nbc,ncd->nbd", grad_scores, key_b, preferred_element_type=jnp.float32
    ) + jnp.einsum("nbv,ndv->nbd", grad_b, kv_used, preferred_element_type=jnp.float32)
    key_grad = jnp.einsum(
        "nbc,nbd->ncd", grad_scores, query_b, preferred_element_type=jnp.float32
    ) + jnp.einsum("ncv,ndv->ncd", value_b, back_used, preferred_element_type=jnp.float32)
    value_grad = jnp.einsum(
        "nbc,nbv->ncv", weights, grad_b, preferred_element_type=jnp.float32
    ) + jnp.einsum("ncd,ndv->ncv", key_b, back_used, preferred_element_type=jnp.float32)
    shape = (half_rows, width)
    return (
        attended.reshape(shape),
        query_grad.astype(jnp.bfloat16).reshape(shape),
        key_grad.astype(jnp.bfloat16).reshape(shape),
        value_grad.astype(jnp.bfloat16).reshape(shape),
    )


def solution(mesh):
    return jax.shard_map(
        per_device,
        mesh=mesh,
        in_specs=(P("seq", "inner"), P("seq", "inner"), P("seq", "inner"), P("seq", "inner")),
        out_specs=(P("seq", "inner"), P("seq", "inner"), P("seq", "inner"), P("seq", "inner")),
        check_vma=False,
    )
```

profile of v0, /device:TPU:0, one launch (start us, length us, event | category | flops | bytes accessed | tf_op | source)
XLA Modules:
  0.0 35.5 jit_solution(14390664379697777175)
XLA Ops:
  0.6 0.0 copy-start
  0.6 0.0 copy-start.1
  0.7 0.0 copy-start.2
  0.7 1.2 %multiply_convert_fusion = bf16[1024,128]{1,0:T(8,128)(2,1)S(1)} fusion(bf16[1024,128]{1,0:T(8,128)(2,1)} %param.11, f32[1024]{0:T(1024)S(1)} %multiply_rsqrt_fusion), kind=kLoop, calls=%fused_computation.19 | loop fusion | flops 393216 | bytes 528384 | tf_op jit(solution)/shard_map/convert_element_type | solution.py:42
  1.9 0.0 copy-done
  1.9 0.9 %fusion.6 = (f32[128,128]{0,1:T(8,128)S(1)}, f32[2,128,128]{1,2,0:T(8,128)}) fusion(bf16[2,512,128]{2,1,0:T(8,128)(2,1)S(1)} %bitcast.56, bf16[2,512,128]{2,1,0:T(8,128)(2,1)S(1)} %bitcast.55), kind=kOutput, calls=%fused_computation.27 | convolution fusion | flops 33570816 | bytes 720896 | tf_op jit(solution)/shard_map/nbd,nbv->ndv/dot_general | solution.py:49
  2.9 0.0 copy-start.4
  2.9 0.1 copy.41
  3.0 0.5 %collective-permute-start.1 = (f32[128,128]{1,0:T(8,128)S(1)}, f32[128,128]{1,0:T(8,128)S(1)}, u32[]{:S(2)}, u32[]{:S(2)}) collective-permute-start(f32[128,128]{1,0:T(8,128)S(1)} %copy.41), channel_id=1, source_target_pairs={{0,1},{1,0},{2,3},{3,2},{4,5},{5,4},{6,7},{7,6},{8,9},{9,8},{10,11... | collective-permute-start | bytes 196616 | tf_op jit(solution)/shard_map/ppermute | solution.py:12
  3.5 0.0 copy-done.1
  3.5 0.0 copy-done.2
  3.5 1.6 %fusion.5 = (f32[128,128]{1,0:T(8,128)}, f32[2,128,128]{2,1,0:T(8,128)}) fusion(bf16[2,512,128]{2,1,0:T(8,128)(2,1)S(1)} %bitcast.60, bf16[2,512,128]{2,1,0:T(8,128)(2,1)S(1)} %bitcast.64), kind=kOutput, calls=%fused_computation.26 | convolution fusion | flops 33570816 | bytes 720896 | tf_op jit(solution)/shard_map/nbd,nbv->ndv/dot_general | solution.py:48
  5.1 0.1 collective-permute-start
  5.1 0.1 iota_compare_fusion
  5.2 0.0 copy-done.4
  5.2 0.5 %select_convert_fusion = bf16[2,512,512]{2,1,0:T(8,128)(2,1)S(1)} fusion(bf16[2,512,128]{2,1,0:T(8,128)(2,1)S(1)} %bitcast.57, bf16[2,512,128]{2,1,0:T(8,128)(2,1)S(1)} %bitcast.65, pred[512,512]{1,0:T(8,128)(4,1)S(1)} %iota_compare_fusion), kind=kOutput, calls=%fused_computation.2 | convolution fusion | flops 135266304 | bytes 1835008 | tf_op jit(solution)/shard_map/nbv,ncv->nbc/dot_general | solution.py:70
  5.7 0.5 %select_convert_fusion.1 = bf16[2,512,512]{2,1,0:T(8,128)(2,1)S(1)} fusion(bf16[2,512,128]{2,1,0:T(8,128)(2,1)S(1)} %bitcast.52, bf16[2,512,128]{2,1,0:T(8,128)(2,1)S(1)} %bitcast.61, pred[512,512]{1,0:T(8,128)(4,1)S(1)} %iota_compare_fusion), kind=kOutput, calls=%fused_computation.3 | convolution fusion | flops 135266304 | bytes 1835008 | tf_op jit(solution)/shard_map/nbd,ncd->nbc/dot_general | solution.py:64
  6.2 0.0 collective-permute-done.1
  6.2 0.0 copy-start.5
  6.2 0.6 %copy-done.5 = f32[128,128]{1,0:T(8,128)} copy-done((f32[128,128]{1,0:T(8,128)}, f32[128,128]{1,0:T(8,128)S(1)}, u32[]{:S(2)}) %copy-start.5) | copy-done | bytes 65560
  6.8 10.4 %all-gather.1 = f32[512,128]{1,0:T(8,128)S(1)} all-gather(f32[128,128]{1,0:T(8,128)S(1)} %add.125), channel_id=3, replica_groups=mesh['seq'=4,'inner'=8] {'seq'}, dimensions={0}, use_global_device_ids=true | all-gather | bytes 327680 | tf_op jit(solution)/shard_map/all_gather | solution.py:19
  17.3 0.1 while.23
  17.4 0.0 collective-permute-done
  17.4 0.0 copy-start.6
  17.5 0.6 %copy-done.6 = f32[128,128]{1,0:T(8,128)} copy-done((f32[128,128]{1,0:T(8,128)}, f32[128,128]{1,0:T(8,128)S(1)}, u32[]{:S(2)}) %copy-start.6) | copy-done | bytes 65560
  18.1 0.8 %add.111 = f32[128,128]{1,0:T(8,128)S(1)} add(f32[128,128]{1,0:T(8,128)} %get-tuple-element.109, f32[128,128]{1,0:T(8,128)S(1)} %collective-permute-done) | non-fusion elementwise | flops 16384 | bytes 196608 | tf_op jit(solution)/shard_map/add | solution.py:54
  18.9 8.9 %all-gather = f32[512,128]{1,0:T(8,128)S(1)} all-gather(f32[128,128]{1,0:T(8,128)S(1)} %add.111), channel_id=2, replica_groups=mesh['seq'=4,'inner'=8] {'seq'}, dimensions={0}, use_global_device_ids=true | all-gather | bytes 327680 | tf_op jit(solution)/shard_map/all_gather | solution.py:19
  27.9 0.9 %select_add_fusion = (f32[128,128]{1,0:T(8,128)S(1)}, f32[128,128]{1,0:T(8,128)S(1)}) fusion(f32[128,128]{1,0:T(8,128)S(1)} %get-tuple-element.84, f32[128,128]{1,0:T(8,128)} %copy-done.5, pred[]{:T(512)S(6)} %eq.5, f32[128,128]{1,0:T(8,128)S(1)} %get-tuple-element.83, f32[128,128]{1,0:T(8,128)} %copy-done.6), kind=kLoop, calls=%fused_computation.22 | loop fusion | flops 65536 | bytes 393217 | tf_op jit(solution)/shard_map/add | solution.py:57
  28.8 0.1 copy.42
  28.8 0.0 copy-start.3
  28.9 1.0 %add_convert_fusion = bf16[2,128,128]{1,2,0:T(8,128)(2,1)S(1)} fusion(f32[128,128]{0,1:T(8,128)S(1)} %copy.42, f32[2,128,128]{1,2,0:T(8,128)} %get-tuple-element.112, f32[128,128]{0,1:T(8,128)} %copy-done.4), kind=kOutput, calls=%fused_computation.20 | output fusion | flops 131072 | bytes 327680 | tf_op jit(solution)/shard_map/jit(cumsum)/reduce_window_sum | solution.py:59
  29.8 0.2 convolution_bitcast_fusion
  30.0 0.2 convolution_bitcast_fusion.2
  30.3 0.0 copy-done.3
  30.3 0.2 fusion.7
  30.5 0.2 convolution_bitcast_fusion.1
  30.8 1.2 %fusion.2 = bf16[2,512,128]{2,1,0:T(8,128)(2,1)} fusion(f32[2,512,128]{2,1,0:T(8,128)S(1)} %convolution_bitcast_fusion, bf16[2,512,512]{2,1,0:T(8,128)(2,1)S(1)} %select_convert_fusion, bf16[2,512,128]{2,1,0:T(8,128)(2,1)S(1)} %bitcast.54), kind=kOutput, calls=%fused_computation.13 | convolution fusion | flops 134479872 | bytes 2097152 | tf_op jit(solution)/shard_map/nbc,nbd->ncd/dot_general | solution.py:75
  32.0 1.1 %fusion.1 = bf16[2,512,128]{2,1,0:T(8,128)(2,1)} fusion(f32[2,512,128]{2,1,0:T(8,128)S(1)} %fusion.7, bf16[2,512,512]{2,1,0:T(8,128)(2,1)S(1)} %select_convert_fusion, bf16[2,512,128]{2,1,0:T(8,128)(2,1)S(1)} %bitcast.63), kind=kOutput, calls=%fused_computation.12 | convolution fusion | flops 134479872 | bytes 2097152 | tf_op jit(solution)/shard_map/nbc,ncd->nbd/dot_general | solution.py:72
  33.1 1.2 %fusion.3 = bf16[2,512,128]{2,1,0:T(8,128)(2,1)} fusion(f32[2,512,128]{2,1,0:T(8,128)S(1)} %convolution_bitcast_fusion.2, bf16[2,512,512]{2,1,0:T(8,128)(2,1)S(1)} %select_convert_fusion.1, bf16[2,512,128]{2,1,0:T(8,128)(2,1)S(1)} %bitcast.59), kind=kOutput, calls=%fused_computation.14 | convolution fusion | flops 134479872 | bytes 2097152 | tf_op jit(solution)/shard_map/nbc,nbv->ncv/dot_general | solution.py:78
  34.4 1.2 %fusion.4 = bf16[2,512,128]{2,1,0:T(8,128)(2,1)} fusion(f32[2,512,128]{2,1,0:T(8,128)S(1)} %convolution_bitcast_fusion.1, bf16[2,512,512]{2,1,0:T(8,128)(2,1)S(1)} %select_convert_fusion.1, bf16[2,512,128]{2,1,0:T(8,128)(2,1)S(1)} %bitcast.67, f32[2,512]{1,0:T(2,128)S(1)} %multiply_rsqrt_fusion.1), kind=kOutput, calls=%fused_computation.15 | convolution fusion | flops 134610944 | bytes 2101248 | tf_op jit(solution)/shard_map/nbc,ncv->nbv/dot_general | solution.py:66
  (10 shorter events, 0.1 us)
Async XLA Ops:
  0.6 1.3 %copy-start = (bf16[1024,128]{1,0:T(8,128)(2,1)S(1)}, bf16[1024,128]{1,0:T(8,128)(2,1)}, u32[]{:S(2)}) copy-start(bf16[1024,128]{1,0:T(8,128)(2,1)} %param.8) | copy-start | bytes 786436
  0.6 2.8 %copy-start.1 = (bf16[1024,128]{1,0:T(8,128)(2,1)S(1)}, bf16[1024,128]{1,0:T(8,128)(2,1)}, u32[]{:S(2)}) copy-start(bf16[1024,128]{1,0:T(8,128)(2,1)} %param.9) | copy-start | bytes 786436
  0.7 2.8 %copy-start.2 = (bf16[1024,128]{1,0:T(8,128)(2,1)S(1)}, bf16[1024,128]{1,0:T(8,128)(2,1)}, u32[]{:S(2)}) copy-start(bf16[1024,128]{1,0:T(8,128)(2,1)} %param.10) | copy-start | bytes 786436
  2.9 2.3 %copy-start.4 = (f32[128,128]{0,1:T(8,128)}, f32[128,128]{0,1:T(8,128)S(1)}, u32[]{:S(2)}) copy-start(f32[128,128]{0,1:T(8,128)S(1)} %get-tuple-element.111) | copy-start | bytes 196612
  3.0 3.2 %collective-permute-start.1 = (f32[128,128]{1,0:T(8,128)S(1)}, f32[128,128]{1,0:T(8,128)S(1)}, u32[]{:S(2)}, u32[]{:S(2)}) collective-permute-start(f32[128,128]{1,0:T(8,128)S(1)} %copy.41), channel_id=1, source_target_pairs={{0,1},{1,0},{2,3},{3,2},{4,5},{5,4},{6,7},{7,6},{8,9},{9,8},{10,11... | collective-permute-start | bytes 196616 | tf_op jit(solution)/shard_map/ppermute | solution.py:12
  5.1 12.4 %collective-permute-start = (f32[128,128]{1,0:T(8,128)}, f32[128,128]{1,0:T(8,128)S(1)}, u32[]{:S(2)}, u32[]{:S(2)}) collective-permute-start(f32[128,128]{1,0:T(8,128)} %get-tuple-element.109), channel_id=1, source_target_pairs={{0,1},{1,0},{2,3},{3,2},{4,5},{5,4},{6,7},{7,6},{8,9},{9,8},{10,11... | collective-permute-start | bytes 196616 | tf_op jit(solution)/shard_map/ppermute | solution.py:12
  6.2 0.6 %copy-start.5 = (f32[128,128]{1,0:T(8,128)}, f32[128,128]{1,0:T(8,128)S(1)}, u32[]{:S(2)}) copy-start(f32[128,128]{1,0:T(8,128)S(1)} %collective-permute-done.1) | copy-start | bytes 196612
  17.4 0.6 %copy-start.6 = (f32[128,128]{1,0:T(8,128)}, f32[128,128]{1,0:T(8,128)S(1)}, u32[]{:S(2)}) copy-start(f32[128,128]{1,0:T(8,128)S(1)} %collective-permute-done) | copy-start | bytes 196612
  28.8 1.4 %copy-start.3 = (f32[2,128,128]{2,1,0:T(8,128)S(1)}, f32[2,128,128]{2,1,0:T(8,128)}, u32[]{:S(2)}) copy-start(f32[2,128,128]{2,1,0:T(8,128)} %get-tuple-element.110) | copy-start | bytes 393220
where the time goes:
time: 35.8 us; the launch traced here: 35.5 us
  blocking collectives  19.4 us (54%)
  matrix products  9.08 us (25%)
  other arithmetic  4.07 us (11%)
  local copies, waits for them, and re-layouts  1.46 us (4%)
  between operations  0.86 us (2%)
  starting transfers between devices  0.58 us (2%)
    all_gather x2, blocking collectives, prefix(): gathered = lax.all_gather(part, axis)  19.4 us
    dot_general x1, matrix products, per_device(): jnp.einsum('nbd,nbv->ndv', key_b, value_b, preferred_element_type=jnp.flo...  1.56 us
    unnamed x14, local copies, waits for them, and re-layouts  1.27 us
    dot_general x1, matrix products, per_device(): jnp.einsum('nbc,nbd->ncd', grad_scores, query_b, preferred_element_type=j...  1.24 us
    dot_general x1, matrix products, per_device(): jnp.einsum('nbc,nbv->ncv', weights, grad_b, preferred_element_type=jnp.fl...  1.23 us
    convert_element_type x1, other arithmetic, per_device(): (scaling[:, None] * out_grad.astype(jnp.float32)).astype(jnp.bfloat16)  1.21 us
    dot_general x1, matrix products, per_device(): jnp.einsum('nbc,ncv->nbv', weights, value_b, preferred_element_type=jnp.f...  1.15 us
    dot_general x1, matrix products, per_device(): jnp.einsum('nbc,ncd->nbd', grad_scores, key_b, preferred_element_type=jnp...  1.14 us
  transfers between devices with their start and end apart: 2, of which 0 were waited for; matrix products, arithmetic and copies ran while one was open for 7% of the time, Pallas kernels for 0%

commit v1 on v0

v1 whole, which is shorter than its diff:
```python
import functools

import jax
import jax.numpy as jnp
from jax import lax
from jax.experimental import pallas as pl
from jax.experimental.pallas import tpu as pltpu
from jax.sharding import PartitionSpec as P

MESH = pl.DeviceIdType.MESH
CHUNK = 256
F32 = jnp.float32
BF16 = jnp.bfloat16


def dot(a, b):
    return lax.dot_general(a, b, (((1,), (0,)), ((), ())), preferred_element_type=F32)


def dot_bt(a, b):
    return lax.dot_general(a, b, (((1,), (1,)), ((), ())), preferred_element_type=F32)


def dot_at(a, b):
    return lax.dot_general(a, b, (((0,), (0,)), ((), ())), preferred_element_type=F32)


def xor(index, mask):
    bit = 1
    out = index
    while bit <= mask:
        if mask & bit:
            out = out + bit - 2 * bit * ((index // bit) % 2)
        bit *= 2
    return out


def kernel(
    n_seq,
    q_hbm, k_hbm, v_hbm, o_hbm,
    att_out, qg_out, kg_out, vg_out,
    q_ref, k_ref, v_ref, o_ref, sg_ref, scale_ref,
    acc, before, after, own, part, mid, got, state,
    in_sem, send_sem, recv_sem,
):
    rows, width = q_ref.shape
    count = rows // CHUNK
    half = width // 2
    seq = lax.axis_index("seq")
    inner = lax.axis_index("inner")
    side = inner % 2
    partner = {"inner": inner + 1 - 2 * side}
    mine = pl.ds(pl.multiple_of(side * half, half), half)
    masks = sorted(range(1, n_seq), key=lambda m: -bin(m).count("1"))

    loads = [
        pltpu.make_async_copy(src, dst, in_sem.at[i])
        for i, (src, dst) in enumerate(
            ((k_hbm, k_ref), (v_hbm, v_ref), (o_hbm, o_ref), (q_hbm, q_ref))
        )
    ]
    for load in loads:
        load.start()

    barrier = pltpu.get_barrier_semaphore()
    pl.semaphore_signal(barrier, inc=1, device_id=partner, device_id_type=MESH)
    for mask in masks:
        pl.semaphore_signal(
            barrier, inc=1, device_id={"seq": xor(seq, mask)}, device_id_type=MESH
        )

    def chunk(c):
        return pl.ds(c * CHUNK, CHUNK)

    loads[0].wait()
    loads[1].wait()
    total = None
    for c in range(count):
        outer = dot_at(k_ref[chunk(c), :], v_ref[chunk(c), :])
        if c:
            before[c] = total
        total = outer if total is None else total + outer
    own[0] = total
    pl.semaphore_wait(barrier, n_seq)
    to_partner = [
        pltpu.make_async_remote_copy(
            own.at[i], part.at[i], send_sem.at[i], recv_sem.at[i],
            device_id=partner, device_id_type=MESH,
        )
        for i in range(2)
    ]
    to_partner[0].start()

    loads[2].wait()
    loads[3].wait()
    base = (seq * 2 + side) * rows
    total = None
    for c in reversed(range(count)):
        place = lax.broadcasted_iota(jnp.int32, (CHUNK, width), 0) + (base + c * CHUNK)
        scale = lax.rsqrt(width * (place.astype(F32) + 1.0))
        scale_ref[chunk(c), :] = scale
        scaled = (scale * o_ref[chunk(c), :].astype(F32)).astype(BF16)
        sg_ref[chunk(c), :] = scaled
        outer = dot_at(q_ref[chunk(c), :], scaled)
        if c < count - 1:
            after[c] = total
        total = outer if total is None else total + outer
    own[1] = total
    to_partner[1].start()

    causal = lax.broadcasted_iota(jnp.int32, (CHUNK, CHUNK), 0) >= lax.broadcasted_iota(
        jnp.int32, (CHUNK, CHUNK), 1
    )

    def local(c):
        query, key = q_ref[chunk(c), :], k_ref[chunk(c), :]
        value, grad = v_ref[chunk(c), :], sg_ref[chunk(c), :]
        weights = jnp.where(causal, dot_bt(query, key), 0.0).astype(BF16)
        grad_scores = jnp.where(causal, dot_bt(grad, value), 0.0).astype(BF16)
        acc[0, chunk(c), :] = dot(weights, value)
        acc[1, chunk(c), :] = dot(grad_scores, key)
        acc[2, chunk(c), :] = dot_at(grad_scores, query)
        acc[3, chunk(c), :] = dot_at(weights, grad)

    local(0)

    for i in range(2):
        to_partner[i].wait_recv()
        mid[i] = own[i, mine, :] + part[i, mine, :]
    to_peers = []
    for i, mask in enumerate(masks):
        later = (seq // (1 << (mask.bit_length() - 1))) % 2
        copy = pltpu.make_async_remote_copy(
            mid.at[later], got.at[i], send_sem.at[2 + i], recv_sem.at[2 + i],
            device_id={"seq": xor(seq, mask)}, device_id_type=MESH,
        )
        copy.start()
        to_peers.append((mask, copy))

    for c in range(1, count):
        local(c)

    earlier_sum = jnp.zeros((half, width), F32)
    later_sum = jnp.zeros((half, width), F32)
    for i in reversed(range(len(masks))):
        mask, copy = to_peers[i]
        copy.wait_recv()
        later = (seq // (1 << (mask.bit_length() - 1))) % 2
        block = got[i]
        earlier_sum += jnp.where(later == 1, block, 0.0)
        later_sum += jnp.where(later == 1, 0.0, block)
    state[0, mine, :] = earlier_sum
    state[1, mine, :] = later_sum
    halves = pltpu.make_async_remote_copy(
        state.at[:, mine, :], state.at[:, mine, :],
        send_sem.at[1 + n_seq], recv_sem.at[1 + n_seq],
        device_id=partner, device_id_type=MESH,
    )
    halves.start()
    halves.wait_recv()

    state_in = state[0] + jnp.where(side == 1, part[0], 0.0)
    back_in = state[1] + jnp.where(side == 1, 0.0, part[1])
    for c in range(count):
        kv_used = (state_in + before[c] if c else state_in).astype(BF16)
        back_used = (back_in + after[c] if c < count - 1 else back_in).astype(BF16)
        query, key = q_ref[chunk(c), :], k_ref[chunk(c), :]
        value, grad = v_ref[chunk(c), :], sg_ref[chunk(c), :]
        att_out[chunk(c), :] = (
            scale_ref[chunk(c), :] * (acc[0, chunk(c), :] + dot(query, kv_used))
        ).astype(BF16)
        qg_out[chunk(c), :] = (acc[1, chunk(c), :] + dot_bt(grad, kv_used)).astype(BF16)
        kg_out[chunk(c), :] = (acc[2, chunk(c), :] + dot_bt(value, back_used)).astype(BF16)
        vg_out[chunk(c), :] = (acc[3, chunk(c), :] + dot(key, back_used)).astype(BF16)

    for copy in to_partner:
        copy.wait_send()
    for _, copy in to_peers:
        copy.wait_send()
    halves.wait_send()


def per_device(n_seq, queries, key_vectors, value_vectors, out_grad):
    rows, width = queries.shape
    count = rows // CHUNK
    n_sem = n_seq + 2
    return pl.pallas_call(
        functools.partial(kernel, n_seq),
        out_shape=[jax.ShapeDtypeStruct((rows, width), BF16)] * 4,
        in_specs=[pl.BlockSpec(memory_space=pltpu.HBM)] * 4,
        out_specs=[pl.BlockSpec(memory_space=pltpu.VMEM)] * 4,
        scratch_shapes=[
            pltpu.VMEM((rows, width), BF16),
            pltpu.VMEM((rows, width), BF16),
            pltpu.VMEM((rows, width), BF16),
            pltpu.VMEM((rows, width), BF16),
            pltpu.VMEM((rows, width), BF16),
            pltpu.VMEM((rows, width), F32),
            pltpu.VMEM((4, rows, width), F32),
            pltpu.VMEM((count, width, width), F32),
            pltpu.VMEM((count, width, width), F32),
            pltpu.VMEM((2, width, width), F32),
            pltpu.VMEM((2, width, width), F32),
            pltpu.VMEM((2, width // 2, width), F32),
            pltpu.VMEM((n_seq - 1, width // 2, width), F32),
            pltpu.VMEM((2, width, width), F32),
            pltpu.SemaphoreType.DMA((4,)),
            pltpu.SemaphoreType.DMA((n_sem,)),
            pltpu.SemaphoreType.DMA((n_sem,)),
        ],
        compiler_params=pltpu.CompilerParams(
            collective_id=0, has_side_effects=True, vmem_limit_bytes=24 * 2**20
        ),
        name="linear_attention",
    )(queries, key_vectors, value_vectors, out_grad)


def solution(mesh):
    spec = P("seq", "inner")
    return jax.shard_map(
        functools.partial(per_device, mesh.shape["seq"]),
        mesh=mesh,
        in_specs=(spec,) * 4,
        out_specs=(spec,) * 4,
        check_vma=False,
    )
```

time: 35.8 us -> 17.3 us (0.48)
  blocking collectives: 19.4 us -> 0 us
  Pallas kernels: 0 us -> 9.78 us
  matrix products: 9.08 us -> 0 us
  local copies, waits for them, and re-layouts: 1.46 us -> 6.6 us
  other arithmetic: 4.07 us -> 0 us
  starting transfers between devices: 0.58 us -> 0 us
    all_gather x2 -> x0, blocking collectives: 19.4 us -> none  [prefix(): gathered = lax.all_gather(part, axis)]
    pallas_call x0 -> x1, Pallas kernels: none -> 9.78 us  [per_device(): pl.pallas_call(functools.partial(kernel, n_seq), out_shape=[jax.ShapeDtyp...]
    dot_general x12 -> x0, matrix products: 9.08 us -> none  [the longest x1 1.56 us: per_device(): jnp.einsum('nbd,nbv->ndv', key_b, value_b, preferred_element_type=jnp.flo...]
    unnamed x14 -> x12, local copies, waits for them, and re-layouts: 1.27 us -> 6.6 us
    add x6 -> x0, other arithmetic: 1.76 us -> none  [the longest x1 0.87 us: per_device(): back_in = later + jnp.where(is_second, 0.0, other_back)]
    convert_element_type x1 -> x0, other arithmetic: 1.21 us -> none  [per_device(): (scaling[:, None] * out_grad.astype(jnp.float32)).astype(jnp.bfloat16)]
    another operation x2 -> x0, other arithmetic: 0.99 us -> none  [the longest x1 0.96 us: per_device(): jnp.cumsum(outer_back, 0)]
    ppermute x2 -> x0, starting transfers between devices: 0.58 us -> none  [from_partner(): return lax.ppermute(value, axis, pairs)]
  transfers between devices with their start and end apart: 2 -> 0, of which waited for: 0 -> 0; matrix products, arithmetic and copies ran while one was open for 7% -> 0% of each run, Pallas kernels for 0% -> 0%
where the time goes in v1:
time: 17.3 us; the launch traced here: 17 us
  Pallas kernels  9.78 us (57%)
  local copies, waits for them, and re-layouts  6.6 us (38%)
  between operations  0.65 us (4%)
    pallas_call x1, Pallas kernels, per_device(): pl.pallas_call(functools.partial(kernel, n_seq), out_shape=[jax.ShapeDtyp...  9.78 us
    unnamed x12, local copies, waits for them, and re-layouts  6.6 us

profile of v1, /device:TPU:0, one launch (start us, length us, event | category | flops | bytes accessed | tf_op | source)
XLA Modules:
  0.0 17.0 jit_solution(12590017916844389762)
XLA Ops:
  0.6 0.0 copy-start
  0.6 0.9 %copy-done = bf16[1024,128]{1,0:T(8,128)(2,1)S(1)} copy-done((bf16[1024,128]{1,0:T(8,128)(2,1)S(1)}, bf16[1024,128]{1,0:T(8,128)(2,1)}, u32[]{:S(2)}) %copy-start) | copy-done | bytes 262168
  1.6 0.0 copy-start.1
  1.6 0.9 %copy-done.1 = bf16[1024,128]{1,0:T(8,128)(2,1)S(1)} copy-done((bf16[1024,128]{1,0:T(8,128)(2,1)S(1)}, bf16[1024,128]{1,0:T(8,128)(2,1)}, u32[]{:S(2)}) %copy-start.1) | copy-done | bytes 262168
  2.5 0.0 copy-start.2
  2.5 0.9 %copy-done.2 = bf16[1024,128]{1,0:T(8,128)(2,1)S(1)} copy-done((bf16[1024,128]{1,0:T(8,128)(2,1)S(1)}, bf16[1024,128]{1,0:T(8,128)(2,1)}, u32[]{:S(2)}) %copy-start.2) | copy-done | bytes 262168
  3.5 0.0 copy-start.3
  3.5 0.9 %copy-done.3 = bf16[1024,128]{1,0:T(8,128)(2,1)S(1)} copy-done((bf16[1024,128]{1,0:T(8,128)(2,1)S(1)}, bf16[1024,128]{1,0:T(8,128)(2,1)}, u32[]{:S(2)}) %copy-start.3) | copy-done | bytes 262168
  4.4 9.8 %linear_attention.1 = (bf16[1024,128]{1,0:T(8,128)(2,1)S(1)}, bf16[1024,128]{1,0:T(8,128)(2,1)S(1)}, bf16[1024,128]{1,0:T(8,128)(2,1)S(1)}, bf16[1024,128]{1,0:T(8,128)(2,1)S(1)}) custom-call(bf16[1024,128]{1,0:T(8,128)(2,1)S(1)} %copy-done, bf16[1024,128]{1,0:T(8,128)(2,1)S(1)} %copy-done.1, bf16[1024,128]{1,0:T(8,128)(2,1)S(1)} %copy-done.2, ...), custom_call_target="tpu_custom_call" | custom-call | tf_op jit(solution)/shard_map/linear_attention/pallas_call | solution.py:187
  14.2 0.7 %copy.12 = bf16[1024,128]{1,0:T(8,128)(2,1)} copy(bf16[1024,128]{1,0:T(8,128)(2,1)S(1)} %get-tuple-element.8) | data formatting | bytes 524288
  14.9 0.7 %copy.13 = bf16[1024,128]{1,0:T(8,128)(2,1)} copy(bf16[1024,128]{1,0:T(8,128)(2,1)S(1)} %get-tuple-element.9) | data formatting | bytes 524288
  15.6 0.7 %copy.14 = bf16[1024,128]{1,0:T(8,128)(2,1)} copy(bf16[1024,128]{1,0:T(8,128)(2,1)S(1)} %get-tuple-element.10) | data formatting | bytes 524288
  16.3 0.7 %copy.15 = bf16[1024,128]{1,0:T(8,128)(2,1)} copy(bf16[1024,128]{1,0:T(8,128)(2,1)S(1)} %get-tuple-element.11) | data formatting | bytes 524288
Async XLA Ops:
  0.6 1.0 %copy-start = (bf16[1024,128]{1,0:T(8,128)(2,1)S(1)}, bf16[1024,128]{1,0:T(8,128)(2,1)}, u32[]{:S(2)}) copy-start(bf16[1024,128]{1,0:T(8,128)(2,1)} %q_hbm.1) | copy-start | bytes 786436
  1.6 0.9 %copy-start.1 = (bf16[1024,128]{1,0:T(8,128)(2,1)S(1)}, bf16[1024,128]{1,0:T(8,128)(2,1)}, u32[]{:S(2)}) copy-start(bf16[1024,128]{1,0:T(8,128)(2,1)} %k_hbm.1) | copy-start | bytes 786436
  2.5 0.9 %copy-start.2 = (bf16[1024,128]{1,0:T(8,128)(2,1)S(1)}, bf16[1024,128]{1,0:T(8,128)(2,1)}, u32[]{:S(2)}) copy-start(bf16[1024,128]{1,0:T(8,128)(2,1)} %v_hbm.1) | copy-start | bytes 786436
  3.5 0.9 %copy-start.3 = (bf16[1024,128]{1,0:T(8,128)(2,1)S(1)}, bf16[1024,128]{1,0:T(8,128)(2,1)}, u32[]{:S(2)}) copy-start(bf16[1024,128]{1,0:T(8,128)(2,1)} %o_hbm.1) | copy-start | bytes 786436

commit v2 on v1

--- a/solution.py
+++ b/solution.py
@@ -35,12 +35,11 @@
     return out
 
 
-def kernel(
+def exchange_kernel(
     n_seq,
     q_hbm, k_hbm, v_hbm, o_hbm,
-    att_out, qg_out, kg_out, vg_out,
-    q_ref, k_ref, v_ref, o_ref, sg_ref, scale_ref,
-    acc, before, after, own, part, mid, got, state,
+    q_ref, k_ref, v_ref, sg_ref, scale_ref, acc, before, after, entering,
+    o_ref, own, part, mid, got, state,
     in_sem, send_sem, recv_sem,
 ):
     rows, width = q_ref.shape
@@ -77,8 +76,7 @@
     total = None
     for c in range(count):
         outer = dot_at(k_ref[chunk(c), :], v_ref[chunk(c), :])
-        if c:
-            before[c] = total
+        before[c] = jnp.zeros_like(outer) if total is None else total
         total = outer if total is None else total + outer
     own[0] = total
     pl.semaphore_wait(barrier, n_seq)
@@ -102,8 +100,7 @@
         scaled = (scale * o_ref[chunk(c), :].astype(F32)).astype(BF16)
         sg_ref[chunk(c), :] = scaled
         outer = dot_at(q_ref[chunk(c), :], scaled)
-        if c < count - 1:
-            after[c] = total
+        after[c] = jnp.zeros_like(outer) if total is None else total
         total = outer if total is None else total + outer
     own[1] = total
     to_partner[1].start()
@@ -159,19 +156,8 @@
     halves.start()
     halves.wait_recv()
 
-    state_in = state[0] + jnp.where(side == 1, part[0], 0.0)
-    back_in = state[1] + jnp.where(side == 1, 0.0, part[1])
-    for c in range(count):
-        kv_used = (state_in + before[c] if c else state_in).astype(BF16)
-        back_used = (back_in + after[c] if c < count - 1 else back_in).astype(BF16)
-        query, key = q_ref[chunk(c), :], k_ref[chunk(c), :]
-        value, grad = v_ref[chunk(c), :], sg_ref[chunk(c), :]
-        att_out[chunk(c), :] = (
-            scale_ref[chunk(c), :] * (acc[0, chunk(c), :] + dot(query, kv_used))
-        ).astype(BF16)
-        qg_out[chunk(c), :] = (acc[1, chunk(c), :] + dot_bt(grad, kv_used)).astype(BF16)
-        kg_out[chunk(c), :] = (acc[2, chunk(c), :] + dot_bt(value, back_used)).astype(BF16)
-        vg_out[chunk(c), :] = (acc[3, chunk(c), :] + dot(key, back_used)).astype(BF16)
+    entering[0] = state[0] + jnp.where(side == 1, part[0], 0.0)
+    entering[1] = state[1] + jnp.where(side == 1, 0.0, part[1])
 
     for copy in to_partner:
         copy.wait_send()
@@ -180,25 +166,62 @@
     halves.wait_send()
 
 
+def carried_kernel(
+    q_ref, k_ref, v_ref, sg_ref, scale_ref, acc, before, after, entering,
+    att_hbm, qg_hbm, kg_hbm, vg_hbm, out_ref, out_sem,
+):
+    count = q_ref.shape[0] // CHUNK
+    stores = []
+    for c in range(count):
+        rows = pl.ds(c * CHUNK, CHUNK)
+        kv_used = (entering[0] + before[c] if c else entering[0]).astype(BF16)
+        back_used = (entering[1] + after[c] if c < count - 1 else entering[1]).astype(BF16)
+        query, key, value, grad = (x[rows, :] for x in (q_ref, k_ref, v_ref, sg_ref))
+        out_ref[0, rows, :] = (
+            scale_ref[rows, :] * (acc[0, rows, :] + dot(query, kv_used))
+        ).astype(BF16)
+        out_ref[1, rows, :] = (acc[1, rows, :] + dot_bt(grad, kv_used)).astype(BF16)
+        out_ref[2, rows, :] = (acc[2, rows, :] + dot_bt(value, back_used)).astype(BF16)
+        out_ref[3, rows, :] = (acc[3, rows, :] + dot(key, back_used)).astype(BF16)
+        for i, dst in enumerate((att_hbm, qg_hbm, kg_hbm, vg_hbm)):
+            store = pltpu.make_async_copy(
+                out_ref.at[i, rows, :], dst.at[rows, :], out_sem.at[i, c]
+            )
+            store.start()
+            stores.append(store)
+    for store in stores:
+        store.wait()
+
+
 def per_device(n_seq, queries, key_vectors, value_vectors, out_grad):
     rows, width = queries.shape
     count = rows // CHUNK
     n_sem = n_seq + 2
-    return pl.pallas_call(
-        functools.partial(kernel, n_seq),
-        out_shape=[jax.ShapeDtypeStruct((rows, width), BF16)] * 4,
-        in_specs=[pl.BlockSpec(memory_space=pltpu.HBM)] * 4,
-        out_specs=[pl.BlockSpec(memory_space=pltpu.VMEM)] * 4,
+    args = [
+        pltpu.with_memory_space_constraint(x, pltpu.HBM)
+        for x in (queries, key_vectors, value_vectors, out_grad)
+    ]
+    tokens = pltpu.VMEM((rows, width), BF16)
+    held = [
+        ((rows, width), BF16),
+        ((rows, width), BF16),
+        ((rows, width), BF16),
+        ((rows, width), BF16),
+        ((rows, width), F32),
+        ((4, rows, width), F32),
+        ((count, width, width), F32),
+        ((count, width, width), F32),
+        ((2, width, width), F32),
+    ]
+    in_vmem = pl.BlockSpec(memory_space=pltpu.VMEM)
+    in_hbm = pl.BlockSpec(memory_space=pltpu.HBM)
+    local = pl.pallas_call(
+        functools.partial(exchange_kernel, n_seq),
+        out_shape=[pltpu.VMEM(shape, kind) for shape, kind in held],
+        in_specs=[in_hbm] * 4,
+        out_specs=[in_vmem] * len(held),
         scratch_shapes=[
-            pltpu.VMEM((rows, width), BF16),
-            pltpu.VMEM((rows, width), BF16),
-            pltpu.VMEM((rows, width), BF16),
-            pltpu.VMEM((rows, width), BF16),
-            pltpu.VMEM((rows, width), BF16),
-            pltpu.VMEM((rows, width), F32),
-            pltpu.VMEM((4, rows, width), F32),
-            pltpu.VMEM((count, width, width), F32),
-            pltpu.VMEM((count, width, width), F32),
+            tokens,
             pltpu.VMEM((2, width, width), F32),
             pltpu.VMEM((2, width, width), F32),
             pltpu.VMEM((2, width // 2, width), F32),
@@ -211,8 +234,20 @@
         compiler_params=pltpu.CompilerParams(
             collective_id=0, has_side_effects=True, vmem_limit_bytes=24 * 2**20
         ),
-        name="linear_attention",
-    )(queries, key_vectors, value_vectors, out_grad)
+        name="exchange",
+    )(*args)
+    return pl.pallas_call(
+        carried_kernel,
+        out_shape=[pltpu.HBM((rows, width), BF16)] * 4,
+        in_specs=[in_vmem] * len(held),
+        out_specs=[in_hbm] * 4,
+        scratch_shapes=[
+            pltpu.VMEM((4, rows, width), BF16),
+            pltpu.SemaphoreType.DMA((4, count)),
+        ],
+        compiler_params=pltpu.CompilerParams(vmem_limit_bytes=24 * 2**20),
+        name="carried",
+    )(*(pltpu.with_memory_space_constraint(x, pltpu.VMEM) for x in local))
 
 
 def solution(mesh):

time: 17.3 us -> 11.5 us (0.66)
  local copies, waits for them, and re-layouts: 6.6 us -> 0 us
  Pallas kernels: 9.78 us -> 10.7 us
    unnamed x12 -> x0, local copies, waits for them, and re-layouts: 6.6 us -> none
    pallas_call x1 -> x2, Pallas kernels: 9.78 us -> 10.7 us  [the longest x1 9.41 us: per_device(): pl.pallas_call(functools.partial(exchange_kernel, n_seq), out_shape=[pltp...]
where the time goes in v2:
time: 11.5 us; the launch traced here: 11.4 us
  Pallas kernels  10.7 us (93%)
  between operations  0.64 us (6%)
    pallas_call x1, Pallas kernels, per_device(): pl.pallas_call(functools.partial(exchange_kernel, n_seq), out_shape=[pltp...  9.41 us
    pallas_call x1, Pallas kernels, per_device(): pl.pallas_call(carried_kernel, out_shape=[pltpu.HBM((rows, width), BF16)]...  1.32 us

profile of v2, /device:TPU:0, one launch (start us, length us, event | category | flops | bytes accessed | tf_op | source)
XLA Modules:
  0.0 11.4 jit_solution(4286173501573498261)
XLA Ops:
  0.6 9.4 %exchange.1 = (bf16[1024,128]{1,0:T(8,128)(2,1)S(1)}, bf16[1024,128]{1,0:T(8,128)(2,1)S(1)}, bf16[1024,128]{1,0:T(8,128)(2,1)S(1)}, bf16[1024,128]{1,0:T(8,128)(...) custom-call(bf16[1024,128]{1,0:T(8,128)(2,1)} %q_hbm.1, ...), custom_call_target="tpu_custom_call" | custom-call | tf_op jit(solution)/shard_map/exchange/pallas_call | solution.py:218
  10.0 1.3 %carried.1 = (bf16[1024,128]{1,0:T(8,128)(2,1)}, bf16[1024,128]{1,0:T(8,128)(2,1)}, bf16[1024,128]{1,0:T(8,128)(2,1)}, bf16[1024,128]{1,0:T(8,128)(2,1)}) custom-call(bf16[1024,128]{1,0:T(8,128)(2,1)S(1)} %get-tuple-element.13.q_ref, bf16[1024,128]{1,0:T(8,128)(2,1)S(1)} %get-tuple-element.14.k_ref, bf16[1024,128]{1,0:T(8,128)(2,1)S(1)} %get-tuple-element.15.v_ref, ...), custom_call_target="tpu_custom_call" | custom-call | tf_op jit(solution)/shard_map/carried/pallas_call | solution.py:239

commit v3 on v2

--- a/solution.py
+++ b/solution.py
@@ -52,14 +52,18 @@
     mine = pl.ds(pl.multiple_of(side * half, half), half)
     masks = sorted(range(1, n_seq), key=lambda m: -bin(m).count("1"))
 
-    loads = [
-        pltpu.make_async_copy(src, dst, in_sem.at[i])
-        for i, (src, dst) in enumerate(
-            ((k_hbm, k_ref), (v_hbm, v_ref), (o_hbm, o_ref), (q_hbm, q_ref))
-        )
-    ]
-    for load in loads:
-        load.start()
+    def chunk(c):
+        return pl.ds(c * CHUNK, CHUNK)
+
+    def load(src, dst, i, c):
+        copy = pltpu.make_async_copy(src.at[chunk(c), :], dst.at[chunk(c), :], in_sem.at[i, c])
+        copy.start()
+        return copy
+
+    grad_loads = {
+        c: (load(o_hbm, o_ref, 0, c), load(q_hbm, q_ref, 1, c)) for c in reversed(range(count))
+    }
+    key_loads = [(load(k_hbm, k_ref, 2, c), load(v_hbm, v_ref, 3, c)) for c in range(count)]
 
     barrier = pltpu.get_barrier_semaphore()
     pl.semaphore_signal(barrier, inc=1, device_id=partner, device_id_type=MESH)
@@ -68,17 +72,21 @@
             barrier, inc=1, device_id={"seq": xor(seq, mask)}, device_id_type=MESH
         )
 
-    def chunk(c):
-        return pl.ds(c * CHUNK, CHUNK)
-
-    loads[0].wait()
-    loads[1].wait()
+    base = (seq * 2 + side) * rows
+    for c in range(count):
+        place = lax.broadcasted_iota(jnp.int32, (CHUNK, width), 0) + (base + c * CHUNK)
+        scale_ref[chunk(c), :] = lax.rsqrt(width * (place.astype(F32) + 1.0))
+
     total = None
-    for c in range(count):
-        outer = dot_at(k_ref[chunk(c), :], v_ref[chunk(c), :])
-        before[c] = jnp.zeros_like(outer) if total is None else total
+    for c in reversed(range(count)):
+        for copy in grad_loads[c]:
+            copy.wait()
+        scaled = (scale_ref[chunk(c), :] * o_ref[chunk(c), :].astype(F32)).astype(BF16)
+        sg_ref[chunk(c), :] = scaled
+        outer = dot_at(q_ref[chunk(c), :], scaled)
+        after[c] = jnp.zeros_like(outer) if total is None else total
         total = outer if total is None else total + outer
-    own[0] = total
+    own[1] = total
     pl.semaphore_wait(barrier, n_seq)
     to_partner = [
         pltpu.make_async_remote_copy(
@@ -87,23 +95,17 @@
         )
         for i in range(2)
     ]
+    to_partner[1].start()
+
+    total = None
+    for c in range(count):
+        for copy in key_loads[c]:
+            copy.wait()
+        outer = dot_at(k_ref[chunk(c), :], v_ref[chunk(c), :])
+        before[c] = jnp.zeros_like(outer) if total is None else total
+        total = outer if total is None else total + outer
+    own[0] = total
     to_partner[0].start()
-
-    loads[2].wait()
-    loads[3].wait()
-    base = (seq * 2 + side) * rows
-    total = None
-    for c in reversed(range(count)):
-        place = lax.broadcasted_iota(jnp.int32, (CHUNK, width), 0) + (base + c * CHUNK)
-        scale = lax.rsqrt(width * (place.astype(F32) + 1.0))
-        scale_ref[chunk(c), :] = scale
-        scaled = (scale * o_ref[chunk(c), :].astype(F32)).astype(BF16)
-        sg_ref[chunk(c), :] = scaled
-        outer = dot_at(q_ref[chunk(c), :], scaled)
-        after[c] = jnp.zeros_like(outer) if total is None else total
-        total = outer if total is None else total + outer
-    own[1] = total
-    to_partner[1].start()
 
     causal = lax.broadcasted_iota(jnp.int32, (CHUNK, CHUNK), 0) >= lax.broadcasted_iota(
         jnp.int32, (CHUNK, CHUNK), 1
@@ -119,11 +121,6 @@
         acc[2, chunk(c), :] = dot_at(grad_scores, query)
         acc[3, chunk(c), :] = dot_at(weights, grad)
 
-    local(0)
-
-    for i in range(2):
-        to_partner[i].wait_recv()
-        mid[i] = own[i, mine, :] + part[i, mine, :]
     to_peers = []
     for i, mask in enumerate(masks):
         later = (seq // (1 << (mask.bit_length() - 1))) % 2
@@ -131,18 +128,21 @@
             mid.at[later], got.at[i], send_sem.at[2 + i], recv_sem.at[2 + i],
             device_id={"seq": xor(seq, mask)}, device_id_type=MESH,
         )
-        copy.start()
-        to_peers.append((mask, copy))
-
-    for c in range(1, count):
+        to_peers.append((later, copy))
+    for kind in (1, 0):
+        to_partner[kind].wait_recv()
+        mid[kind] = own[kind, mine, :] + part[kind, mine, :]
+        for later, copy in to_peers:
+            pl.when(later == kind)(copy.start)
+
+    for c in range(count - 1):
         local(c)
 
     earlier_sum = jnp.zeros((half, width), F32)
     later_sum = jnp.zeros((half, width), F32)
     for i in reversed(range(len(masks))):
-        mask, copy = to_peers[i]
+        later, copy = to_peers[i]
         copy.wait_recv()
-        later = (seq // (1 << (mask.bit_length() - 1))) % 2
         block = got[i]
         earlier_sum += jnp.where(later == 1, block, 0.0)
         later_sum += jnp.where(later == 1, 0.0, block)
@@ -154,6 +154,7 @@
         device_id=partner, device_id_type=MESH,
     )
     halves.start()
+    local(count - 1)
     halves.wait_recv()
 
     entering[0] = state[0] + jnp.where(side == 1, part[0], 0.0)
@@ -227,7 +228,7 @@
             pltpu.VMEM((2, width // 2, width), F32),
             pltpu.VMEM((n_seq - 1, width // 2, width), F32),
             pltpu.VMEM((2, width, width), F32),
-            pltpu.SemaphoreType.DMA((4,)),
+            pltpu.SemaphoreType.DMA((4, count)),
             pltpu.SemaphoreType.DMA((n_sem,)),
             pltpu.SemaphoreType.DMA((n_sem,)),
         ],

time: 11.5 us -> 12 us (1.043)
  Pallas kernels: 10.7 us -> 11.2 us
    pallas_call x1, Pallas kernels: 9.41 us -> 9.84 us  [per_device(): pl.pallas_call(functools.partial(exchange_kernel, n_seq), out_shape=[pltp...]
where the time goes in v3:
time: 12 us; the launch traced here: 11.8 us
  Pallas kernels  11.2 us (93%)
  between operations  0.64 us (5%)
    pallas_call x1, Pallas kernels, per_device(): pl.pallas_call(functools.partial(exchange_kernel, n_seq), out_shape=[pltp...  9.84 us
    pallas_call x1, Pallas kernels, per_device(): pl.pallas_call(carried_kernel, out_shape=[pltpu.HBM((rows, width), BF16)]...  1.32 us

profile of v3, /device:TPU:0, one launch (start us, length us, event | category | flops | bytes accessed | tf_op | source)
XLA Modules:
  0.0 11.8 jit_solution(11564850158129914024)
XLA Ops:
  0.6 9.8 %exchange.1 = (bf16[1024,128]{1,0:T(8,128)(2,1)S(1)}, bf16[1024,128]{1,0:T(8,128)(2,1)S(1)}, bf16[1024,128]{1,0:T(8,128)(2,1)S(1)}, bf16[1024,128]{1,0:T(8,128)(...) custom-call(bf16[1024,128]{1,0:T(8,128)(2,1)} %q_hbm.1, ...), custom_call_target="tpu_custom_call" | custom-call | tf_op jit(solution)/shard_map/exchange/pallas_call | solution.py:219
  10.5 1.3 %carried.1 = (bf16[1024,128]{1,0:T(8,128)(2,1)}, bf16[1024,128]{1,0:T(8,128)(2,1)}, bf16[1024,128]{1,0:T(8,128)(2,1)}, bf16[1024,128]{1,0:T(8,128)(2,1)}) custom-call(bf16[1024,128]{1,0:T(8,128)(2,1)S(1)} %get-tuple-element.13.q_ref, bf16[1024,128]{1,0:T(8,128)(2,1)S(1)} %get-tuple-element.14.k_ref, bf16[1024,128]{1,0:T(8,128)(2,1)S(1)} %get-tuple-element.15.v_ref, ...), custom_call_target="tpu_custom_call" | custom-call | tf_op jit(solution)/shard_map/carried/pallas_call | solution.py:240

commit v4 on v2

--- a/solution.py
+++ b/solution.py
@@ -39,23 +39,20 @@
     n_seq,
     q_hbm, k_hbm, v_hbm, o_hbm,
     q_ref, k_ref, v_ref, sg_ref, scale_ref, acc, before, after, entering,
-    o_ref, own, part, mid, got, state,
+    o_ref, own, part, mid, got, ship, land,
     in_sem, send_sem, recv_sem,
 ):
     rows, width = q_ref.shape
     count = rows // CHUNK
-    half = width // 2
     seq = lax.axis_index("seq")
-    inner = lax.axis_index("inner")
-    side = inner % 2
-    partner = {"inner": inner + 1 - 2 * side}
-    mine = pl.ds(pl.multiple_of(side * half, half), half)
+    side = lax.axis_index("inner") % 2
+    partner = {"inner": lax.axis_index("inner") + 1 - 2 * side}
     masks = sorted(range(1, n_seq), key=lambda m: -bin(m).count("1"))
 
     loads = [
         pltpu.make_async_copy(src, dst, in_sem.at[i])
         for i, (src, dst) in enumerate(
-            ((k_hbm, k_ref), (v_hbm, v_ref), (o_hbm, o_ref), (q_hbm, q_ref))
+            ((o_hbm, o_ref), (q_hbm, q_ref), (k_hbm, k_ref), (v_hbm, v_ref))
         )
     ]
     for load in loads:
@@ -71,39 +68,50 @@
     def chunk(c):
         return pl.ds(c * CHUNK, CHUNK)
 
+    to_partner = pltpu.make_async_remote_copy(
+        own.at[1 - side], part, send_sem.at[0], recv_sem.at[0],
+        device_id=partner, device_id_type=MESH,
+    )
+    to_peers = []
+    for i, mask in enumerate(masks):
+        earlier = (seq // (1 << (mask.bit_length() - 1))) % 2
+        copy = pltpu.make_async_remote_copy(
+            mid, got.at[i], send_sem.at[2 + i], recv_sem.at[2 + i],
+            device_id={"seq": xor(seq, mask)}, device_id_type=MESH,
+        )
+        to_peers.append((earlier, copy))
+    finished = pltpu.make_async_remote_copy(
+        ship, land, send_sem.at[1], recv_sem.at[1],
+        device_id=partner, device_id_type=MESH,
+    )
+
+    base = (seq * 2 + side) * rows
+    for c in range(count):
+        place = lax.broadcasted_iota(jnp.int32, (CHUNK, width), 0) + (base + c * CHUNK)
+        scale_ref[chunk(c), :] = lax.rsqrt(width * (place.astype(F32) + 1.0))
+
     loads[0].wait()
     loads[1].wait()
+    total = None
+    for c in reversed(range(count)):
+        scaled = (scale_ref[chunk(c), :] * o_ref[chunk(c), :].astype(F32)).astype(BF16)
+        sg_ref[chunk(c), :] = scaled
+        outer = dot_at(q_ref[chunk(c), :], scaled)
+        after[c] = jnp.zeros_like(outer) if total is None else total
+        total = outer if total is None else total + outer
+    own[1] = total
+    pl.semaphore_wait(barrier, n_seq)
+    pl.when(side == 0)(to_partner.start)
+
+    loads[2].wait()
+    loads[3].wait()
     total = None
     for c in range(count):
         outer = dot_at(k_ref[chunk(c), :], v_ref[chunk(c), :])
         before[c] = jnp.zeros_like(outer) if total is None else total
         total = outer if total is None else total + outer
     own[0] = total
-    pl.semaphore_wait(barrier, n_seq)
-    to_partner = [
-        pltpu.make_async_remote_copy(
-            own.at[i], part.at[i], send_sem.at[i], recv_sem.at[i],
-            device_id=partner, device_id_type=MESH,
-        )
-        for i in range(2)
-    ]
-    to_partner[0].start()
-
-    loads[2].wait()
-    loads[3].wait()
-    base = (seq * 2 + side) * rows
-    total = None
-    for c in reversed(range(count)):
-        place = lax.broadcasted_iota(jnp.int32, (CHUNK, width), 0) + (base + c * CHUNK)
-        scale = lax.rsqrt(width * (place.astype(F32) + 1.0))
-        scale_ref[chunk(c), :] = scale
-        scaled = (scale * o_ref[chunk(c), :].astype(F32)).astype(BF16)
-        sg_ref[chunk(c), :] = scaled
-        outer = dot_at(q_ref[chunk(c), :], scaled)
-        after[c] = jnp.zeros_like(outer) if total is None else total
-        total = outer if total is None else total + outer
-    own[1] = total
-    to_partner[1].start()
+    pl.when(side == 1)(to_partner.start)
 
     causal = lax.broadcasted_iota(jnp.int32, (CHUNK, CHUNK), 0) >= lax.broadcasted_iota(
         jnp.int32, (CHUNK, CHUNK), 1
@@ -119,51 +127,36 @@
         acc[2, chunk(c), :] = dot_at(grad_scores, query)
         acc[3, chunk(c), :] = dot_at(weights, grad)
 
+    def send_sum(kind):
+        to_partner.wait_recv()
+        mid[...] = own[kind] + part[...]
+        for earlier, copy in to_peers:
+            pl.when(earlier == kind)(copy.start)
+
+    pl.when(side == 1)(lambda: send_sum(1))
     local(0)
-
-    for i in range(2):
-        to_partner[i].wait_recv()
-        mid[i] = own[i, mine, :] + part[i, mine, :]
-    to_peers = []
-    for i, mask in enumerate(masks):
-        later = (seq // (1 << (mask.bit_length() - 1))) % 2
-        copy = pltpu.make_async_remote_copy(
-            mid.at[later], got.at[i], send_sem.at[2 + i], recv_sem.at[2 + i],
-            device_id={"seq": xor(seq, mask)}, device_id_type=MESH,
-        )
-        copy.start()
-        to_peers.append((mask, copy))
-
+    pl.when(side == 0)(lambda: send_sum(0))
     for c in range(1, count):
         local(c)
 
-    earlier_sum = jnp.zeros((half, width), F32)
-    later_sum = jnp.zeros((half, width), F32)
-    for i in reversed(range(len(masks))):
-        mask, copy = to_peers[i]
-        copy.wait_recv()
-        later = (seq // (1 << (mask.bit_length() - 1))) % 2
-        block = got[i]
-        earlier_sum += jnp.where(later == 1, block, 0.0)
-        later_sum += jnp.where(later == 1, 0.0, block)
-    state[0, mine, :] = earlier_sum
-    state[1, mine, :] = later_sum
-    halves = pltpu.make_async_remote_copy(
-        state.at[:, mine, :], state.at[:, mine, :],
-        send_sem.at[1 + n_seq], recv_sem.at[1 + n_seq],
-        device_id=partner, device_id_type=MESH,
-    )
-    halves.start()
-    halves.wait_recv()
-
-    entering[0] = state[0] + jnp.where(side == 1, part[0], 0.0)
-    entering[1] = state[1] + jnp.where(side == 1, 0.0, part[1])
-
-    for copy in to_partner:
-        copy.wait_send()
-    for _, copy in to_peers:
-        copy.wait_send()
-    halves.wait_send()
+    entering[side] = jnp.zeros((width, width), F32)
+    for i in reversed(range(len(to_peers))):
+        earlier, copy = to_peers[i]
+
+        @pl.when(earlier != side)
+        def _():
+            copy.wait_recv()
+            entering[side] += got[i]
+
+    ship[...] = entering[side] + own[side]
+    finished.start()
+    finished.wait_recv()
+    entering[1 - side] = land[...]
+
+    to_partner.wait_send()
+    for earlier, copy in to_peers:
+        pl.when(earlier == side)(copy.wait_send)
+    finished.wait_send()
 
 
 def carried_kernel(
@@ -196,7 +189,7 @@
 def per_device(n_seq, queries, key_vectors, value_vectors, out_grad):
     rows, width = queries.shape
     count = rows // CHUNK
-    n_sem = n_seq + 2
+    n_sem = n_seq + 1
     args = [
         pltpu.with_memory_space_constraint(x, pltpu.HBM)
         for x in (queries, key_vectors, value_vectors, out_grad)
@@ -223,10 +216,11 @@
         scratch_shapes=[
             tokens,
             pltpu.VMEM((2, width, width), F32),
-            pltpu.VMEM((2, width, width), F32),
-            pltpu.VMEM((2, width // 2, width), F32),
-            pltpu.VMEM((n_seq - 1, width // 2, width), F32),
-            pltpu.VMEM((2, width, width), F32),
+            pltpu.VMEM((width, width), F32),
+            pltpu.VMEM((width, width), F32),
+            pltpu.VMEM((n_seq - 1, width, width), F32),
+            pltpu.VMEM((width, width), F32),
+            pltpu.VMEM((width, width), F32),
             pltpu.SemaphoreType.DMA((4,)),
             pltpu.SemaphoreType.DMA((n_sem,)),
             pltpu.SemaphoreType.DMA((n_sem,)),

time: 11.5 us -> 10.9 us (0.948)
  Pallas kernels: 10.7 us -> 10.1 us
    pallas_call x1, Pallas kernels: 9.41 us -> 8.76 us  [per_device(): pl.pallas_call(functools.partial(exchange_kernel, n_seq), out_shape=[pltp...]
where the time goes in v4:
time: 10.9 us; the launch traced here: 10.7 us
  Pallas kernels  10.1 us (93%)
  between operations  0.64 us (6%)
    pallas_call x1, Pallas kernels, per_device(): pl.pallas_call(functools.partial(exchange_kernel, n_seq), out_shape=[pltp...  8.76 us
    pallas_call x1, Pallas kernels, per_device(): pl.pallas_call(carried_kernel, out_shape=[pltpu.HBM((rows, width), BF16)]...  1.32 us

profile of v4, /device:TPU:0, one launch (start us, length us, event | category | flops | bytes accessed | tf_op | source)
XLA Modules:
  0.0 10.7 jit_solution(3015650525530882934)
XLA Ops:
  0.6 8.8 %exchange.1 = (bf16[1024,128]{1,0:T(8,128)(2,1)S(1)}, bf16[1024,128]{1,0:T(8,128)(2,1)S(1)}, bf16[1024,128]{1,0:T(8,128)(2,1)S(1)}, bf16[1024,128]{1,0:T(8,128)(...) custom-call(bf16[1024,128]{1,0:T(8,128)(2,1)} %q_hbm.1, ...), custom_call_target="tpu_custom_call" | custom-call | tf_op jit(solution)/shard_map/exchange/pallas_call | solution.py:211
  9.4 1.3 %carried.1 = (bf16[1024,128]{1,0:T(8,128)(2,1)}, bf16[1024,128]{1,0:T(8,128)(2,1)}, bf16[1024,128]{1,0:T(8,128)(2,1)}, bf16[1024,128]{1,0:T(8,128)(2,1)}) custom-call(bf16[1024,128]{1,0:T(8,128)(2,1)S(1)} %get-tuple-element.13.q_ref, bf16[1024,128]{1,0:T(8,128)(2,1)S(1)} %get-tuple-element.14.k_ref, bf16[1024,128]{1,0:T(8,128)(2,1)S(1)} %get-tuple-element.15.v_ref, ...), custom_call_target="tpu_custom_call" | custom-call | tf_op jit(solution)/shard_map/carried/pallas_call | solution.py:233

commit v5 on v4

--- a/solution.py
+++ b/solution.py
@@ -100,8 +100,11 @@
         after[c] = jnp.zeros_like(outer) if total is None else total
         total = outer if total is None else total + outer
     own[1] = total
-    pl.semaphore_wait(barrier, n_seq)
-    pl.when(side == 0)(to_partner.start)
+
+    @pl.when(seq == n_seq - 1)
+    def _():
+        pl.semaphore_wait(barrier, n_seq)
+        pl.when(side == 0)(to_partner.start)
 
     loads[2].wait()
     loads[3].wait()
@@ -111,6 +114,12 @@
         before[c] = jnp.zeros_like(outer) if total is None else total
         total = outer if total is None else total + outer
     own[0] = total
+
+    @pl.when(seq != n_seq - 1)
+    def _():
+        pl.semaphore_wait(barrier, n_seq)
+        pl.when(side == 0)(to_partner.start)
+
     pl.when(side == 1)(to_partner.start)
 
     causal = lax.broadcasted_iota(jnp.int32, (CHUNK, CHUNK), 0) >= lax.broadcasted_iota(

time: 10.9 us -> 10.9 us (level)
  no operation moved by 1% of the time
where the time goes in v5:
time: 10.9 us; the launch traced here: 10.8 us
  Pallas kernels  10.1 us (93%)
  between operations  0.64 us (6%)
    pallas_call x1, Pallas kernels, per_device(): pl.pallas_call(functools.partial(exchange_kernel, n_seq), out_shape=[pltp...  8.8 us
    pallas_call x1, Pallas kernels, per_device(): pl.pallas_call(carried_kernel, out_shape=[pltpu.HBM((rows, width), BF16)]...  1.32 us

profile of v5, /device:TPU:0, one launch (start us, length us, event | category | flops | bytes accessed | tf_op | source)
XLA Modules:
  0.0 10.8 jit_solution(3094408112571498184)
XLA Ops:
  0.6 8.8 %exchange.1 = (bf16[1024,128]{1,0:T(8,128)(2,1)S(1)}, bf16[1024,128]{1,0:T(8,128)(2,1)S(1)}, bf16[1024,128]{1,0:T(8,128)(2,1)S(1)}, bf16[1024,128]{1,0:T(8,128)(...) custom-call(bf16[1024,128]{1,0:T(8,128)(2,1)} %q_hbm.1, ...), custom_call_target="tpu_custom_call" | custom-call | tf_op jit(solution)/shard_map/exchange/pallas_call | solution.py:220
  9.4 1.3 %carried.1 = (bf16[1024,128]{1,0:T(8,128)(2,1)}, bf16[1024,128]{1,0:T(8,128)(2,1)}, bf16[1024,128]{1,0:T(8,128)(2,1)}, bf16[1024,128]{1,0:T(8,128)(2,1)}) custom-call(bf16[1024,128]{1,0:T(8,128)(2,1)S(1)} %get-tuple-element.13.q_ref, bf16[1024,128]{1,0:T(8,128)(2,1)S(1)} %get-tuple-element.14.k_ref, bf16[1024,128]{1,0:T(8,128)(2,1)S(1)} %get-tuple-element.15.v_ref, ...), custom_call_target="tpu_custom_call" | custom-call | tf_op jit(solution)/shard_map/carried/pallas_call | solution.py:242

commit v6 on v5

--- a/solution.py
+++ b/solution.py
@@ -90,6 +90,22 @@
         place = lax.broadcasted_iota(jnp.int32, (CHUNK, width), 0) + (base + c * CHUNK)
         scale_ref[chunk(c), :] = lax.rsqrt(width * (place.astype(F32) + 1.0))
 
+    row_ids = lax.broadcasted_iota(jnp.int32, (CHUNK, CHUNK), 0)
+    column_ids = lax.broadcasted_iota(jnp.int32, (CHUNK, CHUNK), 1)
+    causal, causal_t = row_ids >= column_ids, row_ids <= column_ids
+
+    def local(c):
+        query, key = q_ref[chunk(c), :], k_ref[chunk(c), :]
+        value, grad = v_ref[chunk(c), :], sg_ref[chunk(c), :]
+        weights = jnp.where(causal, dot_bt(query, key), 0.0).astype(BF16)
+        acc[0, chunk(c), :] = dot(weights, value)
+        grad_scores = jnp.where(causal, dot_bt(grad, value), 0.0).astype(BF16)
+        acc[1, chunk(c), :] = dot(grad_scores, key)
+        grad_scores_t = jnp.where(causal_t, dot_bt(value, grad), 0.0).astype(BF16)
+        acc[2, chunk(c), :] = dot(grad_scores_t, query)
+        weights_t = jnp.where(causal_t, dot_bt(key, query), 0.0).astype(BF16)
+        acc[3, chunk(c), :] = dot(weights_t, grad)
+
     loads[0].wait()
     loads[1].wait()
     total = None
@@ -115,26 +131,19 @@
         total = outer if total is None else total + outer
     own[0] = total
 
+    ahead = count // 2
+
+    @pl.when(seq == 0)
+    def _():
+        for c in range(ahead):
+            local(c)
+
     @pl.when(seq != n_seq - 1)
     def _():
         pl.semaphore_wait(barrier, n_seq)
         pl.when(side == 0)(to_partner.start)
 
     pl.when(side == 1)(to_partner.start)
-
-    causal = lax.broadcasted_iota(jnp.int32, (CHUNK, CHUNK), 0) >= lax.broadcasted_iota(
-        jnp.int32, (CHUNK, CHUNK), 1
-    )
-
-    def local(c):
-        query, key = q_ref[chunk(c), :], k_ref[chunk(c), :]
-        value, grad = v_ref[chunk(c), :], sg_ref[chunk(c), :]
-        weights = jnp.where(causal, dot_bt(query, key), 0.0).astype(BF16)
-        grad_scores = jnp.where(causal, dot_bt(grad, value), 0.0).astype(BF16)
-        acc[0, chunk(c), :] = dot(weights, value)
-        acc[1, chunk(c), :] = dot(grad_scores, key)
-        acc[2, chunk(c), :] = dot_at(grad_scores, query)
-        acc[3, chunk(c), :] = dot_at(weights, grad)
 
     def send_sum(kind):
         to_partner.wait_recv()
@@ -143,9 +152,19 @@
             pl.when(earlier == kind)(copy.start)
 
     pl.when(side == 1)(lambda: send_sum(1))
-    local(0)
+
+    @pl.when(seq != 0)
+    def _():
+        local(0)
+
     pl.when(side == 0)(lambda: send_sum(0))
-    for c in range(1, count):
+
+    @pl.when(seq != 0)
+    def _():
+        for c in range(1, ahead):
+            local(c)
+
+    for c in range(ahead, count):
         local(c)
 
     entering[side] = jnp.zeros((width, width), F32)

time: 10.9 us -> 10.9 us (level)
  no operation moved by 1% of the time
where the time goes in v6:
time: 10.9 us; the launch traced here: 10.8 us
  Pallas kernels  10.1 us (93%)
  between operations  0.64 us (6%)
    pallas_call x1, Pallas kernels, per_device(): pl.pallas_call(functools.partial(exchange_kernel, n_seq), out_shape=[pltp...  8.8 us
    pallas_call x1, Pallas kernels, per_device(): pl.pallas_call(carried_kernel, out_shape=[pltpu.HBM((rows, width), BF16)]...  1.32 us

profile of v6, /device:TPU:0, one launch (start us, length us, event | category | flops | bytes accessed | tf_op | source)
XLA Modules:
  0.0 10.8 jit_solution(14490640501725033250)
XLA Ops:
  0.6 8.8 %exchange.1 = (bf16[1024,128]{1,0:T(8,128)(2,1)S(1)}, bf16[1024,128]{1,0:T(8,128)(2,1)S(1)}, bf16[1024,128]{1,0:T(8,128)(2,1)S(1)}, bf16[1024,128]{1,0:T(8,128)(...) custom-call(bf16[1024,128]{1,0:T(8,128)(2,1)} %q_hbm.1, ...), custom_call_target="tpu_custom_call" | custom-call | tf_op jit(solution)/shard_map/exchange/pallas_call | solution.py:239
  9.4 1.3 %carried.1 = (bf16[1024,128]{1,0:T(8,128)(2,1)}, bf16[1024,128]{1,0:T(8,128)(2,1)}, bf16[1024,128]{1,0:T(8,128)(2,1)}, bf16[1024,128]{1,0:T(8,128)(2,1)}) custom-call(bf16[1024,128]{1,0:T(8,128)(2,1)S(1)} %get-tuple-element.13.q_ref, bf16[1024,128]{1,0:T(8,128)(2,1)S(1)} %get-tuple-element.14.k_ref, bf16[1024,128]{1,0:T(8,128)(2,1)S(1)} %get-tuple-element.15.v_ref, ...), custom_call_target="tpu_custom_call" | custom-call | tf_op jit(solution)/shard_map/carried/pallas_call | solution.py:261

commit v7 on v6

--- a/solution.py
+++ b/solution.py
@@ -49,14 +49,21 @@
     partner = {"inner": lax.axis_index("inner") + 1 - 2 * side}
     masks = sorted(range(1, n_seq), key=lambda m: -bin(m).count("1"))
 
+    cut = rows // 2
     loads = [
-        pltpu.make_async_copy(src, dst, in_sem.at[i])
+        [
+            pltpu.make_async_copy(
+                src.at[pl.ds(p * cut, cut), :], dst.at[pl.ds(p * cut, cut), :], in_sem.at[i, p]
+            )
+            for p in range(2)
+        ]
         for i, (src, dst) in enumerate(
             ((o_hbm, o_ref), (q_hbm, q_ref), (k_hbm, k_ref), (v_hbm, v_ref))
         )
     ]
-    for load in loads:
-        load.start()
+    for pair in loads:
+        for load in pair:
+            load.start()
 
     barrier = pltpu.get_barrier_semaphore()
     pl.semaphore_signal(barrier, inc=1, device_id=partner, device_id_type=MESH)
@@ -68,8 +75,9 @@
     def chunk(c):
         return pl.ds(c * CHUNK, CHUNK)
 
+    owned = 1 - side
     to_partner = pltpu.make_async_remote_copy(
-        own.at[1 - side], part, send_sem.at[0], recv_sem.at[0],
+        own.at[side], part, send_sem.at[0], recv_sem.at[0],
         device_id=partner, device_id_type=MESH,
     )
     to_peers = []
@@ -106,8 +114,10 @@
         weights_t = jnp.where(causal_t, dot_bt(key, query), 0.0).astype(BF16)
         acc[3, chunk(c), :] = dot(weights_t, grad)
 
-    loads[0].wait()
-    loads[1].wait()
+    for load in loads[0]:
+        load.wait()
+    for load in loads[1]:
+        load.wait()
     total = None
     for c in reversed(range(count)):
         scaled = (scale_ref[chunk(c), :] * o_ref[chunk(c), :].astype(F32)).astype(BF16)
@@ -120,10 +130,12 @@
     @pl.when(seq == n_seq - 1)
     def _():
         pl.semaphore_wait(barrier, n_seq)
-        pl.when(side == 0)(to_partner.start)
-
-    loads[2].wait()
-    loads[3].wait()
+        pl.when(side == 1)(to_partner.start)
+
+    for load in loads[2]:
+        load.wait()
+    for load in loads[3]:
+        load.wait()
     total = None
     for c in range(count):
         outer = dot_at(k_ref[chunk(c), :], v_ref[chunk(c), :])
@@ -141,9 +153,9 @@
     @pl.when(seq != n_seq - 1)
     def _():
         pl.semaphore_wait(barrier, n_seq)
-        pl.when(side == 0)(to_partner.start)
-
-    pl.when(side == 1)(to_partner.start)
+        pl.when(side == 1)(to_partner.start)
+
+    pl.when(side == 0)(to_partner.start)
 
     def send_sum(kind):
         to_partner.wait_recv()
@@ -151,13 +163,13 @@
         for earlier, copy in to_peers:
             pl.when(earlier == kind)(copy.start)
 
-    pl.when(side == 1)(lambda: send_sum(1))
+    pl.when(side == 0)(lambda: send_sum(1))
 
     @pl.when(seq != 0)
     def _():
         local(0)
 
-    pl.when(side == 0)(lambda: send_sum(0))
+    pl.when(side == 1)(lambda: send_sum(0))
 
     @pl.when(seq != 0)
     def _():
@@ -167,23 +179,23 @@
     for c in range(ahead, count):
         local(c)
 
-    entering[side] = jnp.zeros((width, width), F32)
+    ship[...] = jnp.zeros((width, width), F32)
     for i in reversed(range(len(to_peers))):
         earlier, copy = to_peers[i]
 
-        @pl.when(earlier != side)
+        @pl.when(earlier != owned)
         def _():
             copy.wait_recv()
-            entering[side] += got[i]
-
-    ship[...] = entering[side] + own[side]
+            ship[...] += got[i]
+
     finished.start()
+    entering[owned] = ship[...] + part[...]
     finished.wait_recv()
-    entering[1 - side] = land[...]
+    entering[side] = land[...]
 
     to_partner.wait_send()
     for earlier, copy in to_peers:
-        pl.when(earlier == side)(copy.wait_send)
+        pl.when(earlier == owned)(copy.wait_send)
     finished.wait_send()
 
 
@@ -249,7 +261,7 @@
             pltpu.VMEM((n_seq - 1, width, width), F32),
             pltpu.VMEM((width, width), F32),
             pltpu.VMEM((width, width), F32),
-            pltpu.SemaphoreType.DMA((4,)),
+            pltpu.SemaphoreType.DMA((4, 2)),
             pltpu.SemaphoreType.DMA((n_sem,)),
             pltpu.SemaphoreType.DMA((n_sem,)),
         ],

time: 10.9 us -> 11.3 us (1.037)
  Pallas kernels: 10.1 us -> 10.6 us
    pallas_call x1, Pallas kernels: 8.8 us -> 9.23 us  [per_device(): pl.pallas_call(functools.partial(exchange_kernel, n_seq), out_shape=[pltp...]
where the time goes in v7:
time: 11.3 us; the launch traced here: 11.2 us
  Pallas kernels  10.6 us (94%)
  between operations  0.64 us (6%)
    pallas_call x1, Pallas kernels, per_device(): pl.pallas_call(functools.partial(exchange_kernel, n_seq), out_shape=[pltp...  9.23 us
    pallas_call x1, Pallas kernels, per_device(): pl.pallas_call(carried_kernel, out_shape=[pltpu.HBM((rows, width), BF16)]...  1.32 us

profile of v7, /device:TPU:0, one launch (start us, length us, event | category | flops | bytes accessed | tf_op | source)
XLA Modules:
  0.0 11.2 jit_solution(10361353569724310448)
XLA Ops:
  0.6 9.2 %exchange.1 = (bf16[1024,128]{1,0:T(8,128)(2,1)S(1)}, bf16[1024,128]{1,0:T(8,128)(2,1)S(1)}, bf16[1024,128]{1,0:T(8,128)(2,1)S(1)}, bf16[1024,128]{1,0:T(8,128)(...) custom-call(bf16[1024,128]{1,0:T(8,128)(2,1)} %q_hbm.1, ...), custom_call_target="tpu_custom_call" | custom-call | tf_op jit(solution)/shard_map/exchange/pallas_call | solution.py:251
  9.9 1.3 %carried.1 = (bf16[1024,128]{1,0:T(8,128)(2,1)}, bf16[1024,128]{1,0:T(8,128)(2,1)}, bf16[1024,128]{1,0:T(8,128)(2,1)}, bf16[1024,128]{1,0:T(8,128)(2,1)}) custom-call(bf16[1024,128]{1,0:T(8,128)(2,1)S(1)} %get-tuple-element.13.q_ref, bf16[1024,128]{1,0:T(8,128)(2,1)S(1)} %get-tuple-element.14.k_ref, bf16[1024,128]{1,0:T(8,128)(2,1)S(1)} %get-tuple-element.15.v_ref, ...), custom_call_target="tpu_custom_call" | custom-call | tf_op jit(solution)/shard_map/carried/pallas_call | solution.py:273

commit v8 on v7

--- a/solution.py
+++ b/solution.py
@@ -49,21 +49,14 @@
     partner = {"inner": lax.axis_index("inner") + 1 - 2 * side}
     masks = sorted(range(1, n_seq), key=lambda m: -bin(m).count("1"))
 
-    cut = rows // 2
     loads = [
-        [
-            pltpu.make_async_copy(
-                src.at[pl.ds(p * cut, cut), :], dst.at[pl.ds(p * cut, cut), :], in_sem.at[i, p]
-            )
-            for p in range(2)
-        ]
+        pltpu.make_async_copy(src, dst, in_sem.at[i])
         for i, (src, dst) in enumerate(
             ((o_hbm, o_ref), (q_hbm, q_ref), (k_hbm, k_ref), (v_hbm, v_ref))
         )
     ]
-    for pair in loads:
-        for load in pair:
-            load.start()
+    loads[0].start()
+    loads[1].start()
 
     barrier = pltpu.get_barrier_semaphore()
     pl.semaphore_signal(barrier, inc=1, device_id=partner, device_id_type=MESH)
@@ -114,10 +107,16 @@
         weights_t = jnp.where(causal_t, dot_bt(key, query), 0.0).astype(BF16)
         acc[3, chunk(c), :] = dot(weights_t, grad)
 
-    for load in loads[0]:
-        load.wait()
-    for load in loads[1]:
-        load.wait()
+    def send_sum(kind):
+        to_partner.wait_recv()
+        mid[...] = own[kind] + part[...]
+        for earlier, copy in to_peers:
+            pl.when(earlier == kind)(copy.start)
+
+    loads[0].wait()
+    loads[1].wait()
+    loads[2].start()
+    loads[3].start()
     total = None
     for c in reversed(range(count)):
         scaled = (scale_ref[chunk(c), :] * o_ref[chunk(c), :].astype(F32)).astype(BF16)
@@ -131,11 +130,10 @@
     def _():
         pl.semaphore_wait(barrier, n_seq)
         pl.when(side == 1)(to_partner.start)
-
-    for load in loads[2]:
-        load.wait()
-    for load in loads[3]:
-        load.wait()
+        pl.when(side == 0)(lambda: send_sum(1))
+
+    loads[2].wait()
+    loads[3].wait()
     total = None
     for c in range(count):
         outer = dot_at(k_ref[chunk(c), :], v_ref[chunk(c), :])
@@ -157,13 +155,7 @@
 
     pl.when(side == 0)(to_partner.start)
 
-    def send_sum(kind):
-        to_partner.wait_recv()
-        mid[...] = own[kind] + part[...]
-        for earlier, copy in to_peers:
-            pl.when(earlier == kind)(copy.start)
-
-    pl.when(side == 0)(lambda: send_sum(1))
+    pl.when((side == 0) & (seq != n_seq - 1))(lambda: send_sum(1))
 
     @pl.when(seq != 0)
     def _():
@@ -261,7 +253,7 @@
             pltpu.VMEM((n_seq - 1, width, width), F32),
             pltpu.VMEM((width, width), F32),
             pltpu.VMEM((width, width), F32),
-            pltpu.SemaphoreType.DMA((4, 2)),
+            pltpu.SemaphoreType.DMA((4,)),
             pltpu.SemaphoreType.DMA((n_sem,)),
             pltpu.SemaphoreType.DMA((n_sem,)),
         ],

time: 11.3 us -> 12 us (1.062)
  Pallas kernels: 10.6 us -> 11.2 us
    pallas_call x1, Pallas kernels: 9.23 us -> 9.86 us  [per_device(): pl.pallas_call(functools.partial(exchange_kernel, n_seq), out_shape=[pltp...]
where the time goes in v8:
time: 12 us; the launch traced here: 11.8 us
  Pallas kernels  11.2 us (93%)
  between operations  0.64 us (5%)
    pallas_call x1, Pallas kernels, per_device(): pl.pallas_call(functools.partial(exchange_kernel, n_seq), out_shape=[pltp...  9.86 us
    pallas_call x1, Pallas kernels, per_device(): pl.pallas_call(carried_kernel, out_shape=[pltpu.HBM((rows, width), BF16)]...  1.32 us

profile of v8, /device:TPU:0, one launch (start us, length us, event | category | flops | bytes accessed | tf_op | source)
XLA Modules:
  0.0 11.8 jit_solution(469156641501738355)
XLA Ops:
  0.6 9.9 %exchange.1 = (bf16[1024,128]{1,0:T(8,128)(2,1)S(1)}, bf16[1024,128]{1,0:T(8,128)(2,1)S(1)}, bf16[1024,128]{1,0:T(8,128)(2,1)S(1)}, bf16[1024,128]{1,0:T(8,128)(...) custom-call(bf16[1024,128]{1,0:T(8,128)(2,1)} %q_hbm.1, ...), custom_call_target="tpu_custom_call" | custom-call | tf_op jit(solution)/shard_map/exchange/pallas_call | solution.py:243
  10.5 1.3 %carried.1 = (bf16[1024,128]{1,0:T(8,128)(2,1)}, bf16[1024,128]{1,0:T(8,128)(2,1)}, bf16[1024,128]{1,0:T(8,128)(2,1)}, bf16[1024,128]{1,0:T(8,128)(2,1)}) custom-call(bf16[1024,128]{1,0:T(8,128)(2,1)S(1)} %get-tuple-element.13.q_ref, bf16[1024,128]{1,0:T(8,128)(2,1)S(1)} %get-tuple-element.14.k_ref, bf16[1024,128]{1,0:T(8,128)(2,1)S(1)} %get-tuple-element.15.v_ref, ...), custom_call_target="tpu_custom_call" | custom-call | tf_op jit(solution)/shard_map/carried/pallas_call | solution.py:265

commit v9 on v6

--- a/solution.py
+++ b/solution.py
@@ -19,10 +19,6 @@
 
 def dot_bt(a, b):
     return lax.dot_general(a, b, (((1,), (1,)), ((), ())), preferred_element_type=F32)
-
-
-def dot_at(a, b):
-    return lax.dot_general(a, b, (((0,), (0,)), ((), ())), preferred_element_type=F32)
 
 
 def xor(index, mask):
@@ -90,6 +86,14 @@
         place = lax.broadcasted_iota(jnp.int32, (CHUNK, width), 0) + (base + c * CHUNK)
         scale_ref[chunk(c), :] = lax.rsqrt(width * (place.astype(F32) + 1.0))
 
+    eye = (
+        lax.broadcasted_iota(jnp.int32, (width, width), 0)
+        == lax.broadcasted_iota(jnp.int32, (width, width), 1)
+    ).astype(F32).astype(BF16)
+
+    def flip(a):
+        return dot_bt(eye, a).astype(BF16)
+
     row_ids = lax.broadcasted_iota(jnp.int32, (CHUNK, CHUNK), 0)
     column_ids = lax.broadcasted_iota(jnp.int32, (CHUNK, CHUNK), 1)
     causal, causal_t = row_ids >= column_ids, row_ids <= column_ids
@@ -112,12 +116,12 @@
     for c in reversed(range(count)):
         scaled = (scale_ref[chunk(c), :] * o_ref[chunk(c), :].astype(F32)).astype(BF16)
         sg_ref[chunk(c), :] = scaled
-        outer = dot_at(q_ref[chunk(c), :], scaled)
+        outer = dot(flip(q_ref[chunk(c), :]), scaled)
         after[c] = jnp.zeros_like(outer) if total is None else total
         total = outer if total is None else total + outer
     own[1] = total
 
-    @pl.when(seq == n_seq - 1)
+    @pl.when(seq != 0)
     def _():
         pl.semaphore_wait(barrier, n_seq)
         pl.when(side == 0)(to_partner.start)
@@ -126,7 +130,7 @@
     loads[3].wait()
     total = None
     for c in range(count):
-        outer = dot_at(k_ref[chunk(c), :], v_ref[chunk(c), :])
+        outer = dot(flip(k_ref[chunk(c), :]), v_ref[chunk(c), :])
         before[c] = jnp.zeros_like(outer) if total is None else total
         total = outer if total is None else total + outer
     own[0] = total
@@ -138,7 +142,7 @@
         for c in range(ahead):
             local(c)
 
-    @pl.when(seq != n_seq - 1)
+    @pl.when(seq == 0)
     def _():
         pl.semaphore_wait(barrier, n_seq)
         pl.when(side == 0)(to_partner.start)

time: 10.9 us -> 11.1 us (1.018)
  Pallas kernels: 10.1 us -> 10.3 us
    pallas_call x1, Pallas kernels: 8.8 us -> 9 us  [per_device(): pl.pallas_call(functools.partial(exchange_kernel, n_seq), out_shape=[pltp...]
where the time goes in v9:
time: 11.1 us; the launch traced here: 11 us
  Pallas kernels  10.3 us (93%)
  between operations  0.64 us (6%)
    pallas_call x1, Pallas kernels, per_device(): pl.pallas_call(functools.partial(exchange_kernel, n_seq), out_shape=[pltp...  9 us
    pallas_call x1, Pallas kernels, per_device(): pl.pallas_call(carried_kernel, out_shape=[pltpu.HBM((rows, width), BF16)]...  1.32 us

profile of v9, /device:TPU:0, one launch (start us, length us, event | category | flops | bytes accessed | tf_op | source)
XLA Modules:
  0.0 11.0 jit_solution(11415648760678238941)
XLA Ops:
  0.6 9.0 %exchange.1 = (bf16[1024,128]{1,0:T(8,128)(2,1)S(1)}, bf16[1024,128]{1,0:T(8,128)(2,1)S(1)}, bf16[1024,128]{1,0:T(8,128)(2,1)S(1)}, bf16[1024,128]{1,0:T(8,128)(...) custom-call(bf16[1024,128]{1,0:T(8,128)(2,1)} %q_hbm.1, ...), custom_call_target="tpu_custom_call" | custom-call | tf_op jit(solution)/shard_map/exchange/pallas_call | solution.py:243
  9.6 1.3 %carried.1 = (bf16[1024,128]{1,0:T(8,128)(2,1)}, bf16[1024,128]{1,0:T(8,128)(2,1)}, bf16[1024,128]{1,0:T(8,128)(2,1)}, bf16[1024,128]{1,0:T(8,128)(2,1)}) custom-call(bf16[1024,128]{1,0:T(8,128)(2,1)S(1)} %get-tuple-element.13.q_ref, bf16[1024,128]{1,0:T(8,128)(2,1)S(1)} %get-tuple-element.14.k_ref, bf16[1024,128]{1,0:T(8,128)(2,1)S(1)} %get-tuple-element.15.v_ref, ...), custom_call_target="tpu_custom_call" | custom-call | tf_op jit(solution)/shard_map/carried/pallas_call | solution.py:265

commit v10 on v5

--- a/solution.py
+++ b/solution.py
@@ -66,7 +66,7 @@
         )
 
     def chunk(c):
-        return pl.ds(c * CHUNK, CHUNK)
+        return pl.ds(pl.multiple_of(c * CHUNK, CHUNK), CHUNK)
 
     to_partner = pltpu.make_async_remote_copy(
         own.at[1 - side], part, send_sem.at[0], recv_sem.at[0],
@@ -86,20 +86,22 @@
     )
 
     base = (seq * 2 + side) * rows
-    for c in range(count):
+    @pl.loop(0, count)
+    def _(c):
         place = lax.broadcasted_iota(jnp.int32, (CHUNK, width), 0) + (base + c * CHUNK)
         scale_ref[chunk(c), :] = lax.rsqrt(width * (place.astype(F32) + 1.0))
 
     loads[0].wait()
     loads[1].wait()
-    total = None
-    for c in reversed(range(count)):
+    own[...] = jnp.zeros(own.shape, F32)
+
+    @pl.loop(0, count)
+    def _(step):
+        c = count - 1 - step
         scaled = (scale_ref[chunk(c), :] * o_ref[chunk(c), :].astype(F32)).astype(BF16)
         sg_ref[chunk(c), :] = scaled
-        outer = dot_at(q_ref[chunk(c), :], scaled)
-        after[c] = jnp.zeros_like(outer) if total is None else total
-        total = outer if total is None else total + outer
-    own[1] = total
+        after[c] = own[1]
+        own[1] += dot_at(q_ref[chunk(c), :], scaled)
 
     @pl.when(seq == n_seq - 1)
     def _():
@@ -108,12 +110,11 @@
 
     loads[2].wait()
     loads[3].wait()
-    total = None
-    for c in range(count):
-        outer = dot_at(k_ref[chunk(c), :], v_ref[chunk(c), :])
-        before[c] = jnp.zeros_like(outer) if total is None else total
-        total = outer if total is None else total + outer
-    own[0] = total
+
+    @pl.loop(0, count)
+    def _(c):
+        before[c] = own[0]
+        own[0] += dot_at(k_ref[chunk(c), :], v_ref[chunk(c), :])
 
     @pl.when(seq != n_seq - 1)
     def _():
@@ -143,10 +144,8 @@
             pl.when(earlier == kind)(copy.start)
 
     pl.when(side == 1)(lambda: send_sum(1))
-    local(0)
     pl.when(side == 0)(lambda: send_sum(0))
-    for c in range(1, count):
-        local(c)
+    pl.loop(0, count)(local)
 
     entering[side] = jnp.zeros((width, width), F32)
     for i in reversed(range(len(to_peers))):
@@ -173,11 +172,13 @@
     att_hbm, qg_hbm, kg_hbm, vg_hbm, out_ref, out_sem,
 ):
     count = q_ref.shape[0] // CHUNK
-    stores = []
-    for c in range(count):
-        rows = pl.ds(c * CHUNK, CHUNK)
-        kv_used = (entering[0] + before[c] if c else entering[0]).astype(BF16)
-        back_used = (entering[1] + after[c] if c < count - 1 else entering[1]).astype(BF16)
+    outs = (att_hbm, qg_hbm, kg_hbm, vg_hbm)
+
+    @pl.loop(0, count)
+    def _(c):
+        rows = pl.ds(pl.multiple_of(c * CHUNK, CHUNK), CHUNK)
+        kv_used = (entering[0] + before[c]).astype(BF16)
+        back_used = (entering[1] + after[c]).astype(BF16)
         query, key, value, grad = (x[rows, :] for x in (q_ref, k_ref, v_ref, sg_ref))
         out_ref[0, rows, :] = (
             scale_ref[rows, :] * (acc[0, rows, :] + dot(query, kv_used))
@@ -185,14 +186,13 @@
         out_ref[1, rows, :] = (acc[1, rows, :] + dot_bt(grad, kv_used)).astype(BF16)
         out_ref[2, rows, :] = (acc[2, rows, :] + dot_bt(value, back_used)).astype(BF16)
         out_ref[3, rows, :] = (acc[3, rows, :] + dot(key, back_used)).astype(BF16)
-        for i, dst in enumerate((att_hbm, qg_hbm, kg_hbm, vg_hbm)):
-            store = pltpu.make_async_copy(
-                out_ref.at[i, rows, :], dst.at[rows, :], out_sem.at[i, c]
-            )
-            store.start()
-            stores.append(store)
-    for store in stores:
-        store.wait()
+        for i, dst in enumerate(outs):
+            pltpu.make_async_copy(
+                out_ref.at[i, rows, :], dst.at[rows, :], out_sem.at[i]
+            ).start()
+
+    for i, dst in enumerate(outs):
+        pltpu.make_async_copy(out_ref.at[i], dst, out_sem.at[i]).wait()
 
 
 def per_device(n_seq, queries, key_vectors, value_vectors, out_grad):
@@ -246,7 +246,7 @@
         out_specs=[in_hbm] * 4,
         scratch_shapes=[
             pltpu.VMEM((4, rows, width), BF16),
-            pltpu.SemaphoreType.DMA((4, count)),
+            pltpu.SemaphoreType.DMA((4,)),
         ],
         compiler_params=pltpu.CompilerParams(vmem_limit_bytes=24 * 2**20),
         name="carried",

time: 10.9 us -> 12.3 us (1.13)
  Pallas kernels: 10.1 us -> 11.5 us
    pallas_call x1, Pallas kernels: 8.8 us -> 9.89 us  [per_device(): pl.pallas_call(functools.partial(exchange_kernel, n_seq), out_shape=[pltp...]
    pallas_call x1, Pallas kernels: 1.32 us -> 1.64 us  [per_device(): pl.pallas_call(carried_kernel, out_shape=[pltpu.HBM((rows, width), BF16)]...]
where the time goes in v10:
time: 12.3 us; the launch traced here: 12.2 us
  Pallas kernels  11.5 us (93%)
  between operations  0.64 us (5%)
    pallas_call x1, Pallas kernels, per_device(): pl.pallas_call(functools.partial(exchange_kernel, n_seq), out_shape=[pltp...  9.89 us
    pallas_call x1, Pallas kernels, per_device(): pl.pallas_call(carried_kernel, out_shape=[pltpu.HBM((rows, width), BF16)]...  1.64 us

profile of v10, /device:TPU:0, one launch (start us, length us, event | category | flops | bytes accessed | tf_op | source)
XLA Modules:
  0.0 12.2 jit_solution(7295308694676703576)
XLA Ops:
  0.6 9.9 %exchange.1 = (bf16[1024,128]{1,0:T(8,128)(2,1)S(1)}, bf16[1024,128]{1,0:T(8,128)(2,1)S(1)}, bf16[1024,128]{1,0:T(8,128)(2,1)S(1)}, bf16[1024,128]{1,0:T(8,128)(...) custom-call(bf16[1024,128]{1,0:T(8,128)(2,1)} %q_hbm.1, ...), custom_call_target="tpu_custom_call" | custom-call | tf_op jit(solution)/shard_map/exchange/pallas_call | solution.py:220
  10.5 1.6 %carried.1 = (bf16[1024,128]{1,0:T(8,128)(2,1)}, bf16[1024,128]{1,0:T(8,128)(2,1)}, bf16[1024,128]{1,0:T(8,128)(2,1)}, bf16[1024,128]{1,0:T(8,128)(2,1)}) custom-call(bf16[1024,128]{1,0:T(8,128)(2,1)S(1)} %get-tuple-element.13.q_ref, bf16[1024,128]{1,0:T(8,128)(2,1)S(1)} %get-tuple-element.14.k_ref, bf16[1024,128]{1,0:T(8,128)(2,1)S(1)} %get-tuple-element.15.v_ref, ...), custom_call_target="tpu_custom_call" | custom-call | tf_op jit(solution)/shard_map/carried/pallas_call | solution.py:242

commit v11 on v6

--- a/solution.py
+++ b/solution.py
@@ -39,7 +39,7 @@
     n_seq,
     q_hbm, k_hbm, v_hbm, o_hbm,
     q_ref, k_ref, v_ref, sg_ref, scale_ref, acc, before, after, entering,
-    o_ref, own, part, mid, got, ship, land,
+    o_ref, own, part, mid, got, extra, ship, land,
     in_sem, send_sem, recv_sem,
 ):
     rows, width = q_ref.shape
@@ -65,6 +65,16 @@
             barrier, inc=1, device_id={"seq": xor(seq, mask)}, device_id_type=MESH
         )
 
+    is_last = seq == n_seq - 1
+    across = {
+        "seq": xor(seq, n_seq - 1),
+        "inner": lax.axis_index("inner") + 1 - 2 * side,
+    }
+
+    @pl.when((seq == 0) & (side == 1))
+    def _():
+        pl.semaphore_signal(barrier, inc=1, device_id=across, device_id_type=MESH)
+
     def chunk(c):
         return pl.ds(c * CHUNK, CHUNK)
 
@@ -80,6 +90,14 @@
             device_id={"seq": xor(seq, mask)}, device_id_type=MESH,
         )
         to_peers.append((earlier, copy))
+    direct = pltpu.make_async_remote_copy(
+        own.at[1], extra, send_sem.at[1 + n_seq], recv_sem.at[1 + n_seq],
+        device_id=across, device_id_type=MESH,
+    )
+    direct_twin = pltpu.make_async_remote_copy(
+        own.at[1], got.at[0], send_sem.at[2], recv_sem.at[2],
+        device_id={"seq": xor(seq, masks[0])}, device_id_type=MESH,
+    )
     finished = pltpu.make_async_remote_copy(
         ship, land, send_sem.at[1], recv_sem.at[1],
         device_id=partner, device_id_type=MESH,
@@ -117,9 +135,11 @@
         total = outer if total is None else total + outer
     own[1] = total
 
-    @pl.when(seq == n_seq - 1)
-    def _():
-        pl.semaphore_wait(barrier, n_seq)
+    @pl.when(is_last)
+    def _():
+        pl.semaphore_wait(barrier, n_seq + 1 - side)
+        pl.when(side == 0)(direct.start)
+        pl.when(side == 1)(direct_twin.start)
         pl.when(side == 0)(to_partner.start)
 
     loads[2].wait()
@@ -148,8 +168,11 @@
     def send_sum(kind):
         to_partner.wait_recv()
         mid[...] = own[kind] + part[...]
-        for earlier, copy in to_peers:
-            pl.when(earlier == kind)(copy.start)
+        for i, (earlier, copy) in enumerate(to_peers):
+            if i == 0:
+                pl.when((earlier == kind) & (seq != n_seq - 1))(copy.start)
+            else:
+                pl.when(earlier == kind)(copy.start)
 
     pl.when(side == 1)(lambda: send_sum(1))
 
@@ -176,12 +199,18 @@
             copy.wait_recv()
             entering[side] += got[i]
 
+    @pl.when((seq == 0) & (side == 1))
+    def _():
+        direct.wait_recv()
+        entering[1] += extra[...]
+
     ship[...] = entering[side] + own[side]
     finished.start()
     finished.wait_recv()
     entering[1 - side] = land[...]
 
     to_partner.wait_send()
+    pl.when(is_last & (side == 0))(direct.wait_send)
     for earlier, copy in to_peers:
         pl.when(earlier == side)(copy.wait_send)
     finished.wait_send()
@@ -217,7 +246,7 @@
 def per_device(n_seq, queries, key_vectors, value_vectors, out_grad):
     rows, width = queries.shape
     count = rows // CHUNK
-    n_sem = n_seq + 1
+    n_sem = n_seq + 2
     args = [
         pltpu.with_memory_space_constraint(x, pltpu.HBM)
         for x in (queries, key_vectors, value_vectors, out_grad)
@@ -249,6 +278,7 @@
             pltpu.VMEM((n_seq - 1, width, width), F32),
             pltpu.VMEM((width, width), F32),
             pltpu.VMEM((width, width), F32),
+            pltpu.VMEM((width, width), F32),
             pltpu.SemaphoreType.DMA((4,)),
             pltpu.SemaphoreType.DMA((n_sem,)),
             pltpu.SemaphoreType.DMA((n_sem,)),

time: 10.9 us -> 11 us (level)
  no operation moved by 1% of the time
where the time goes in v11:
time: 11 us; the launch traced here: 10.8 us
  Pallas kernels  10.2 us (93%)
  between operations  0.64 us (6%)
    pallas_call x1, Pallas kernels, per_device(): pl.pallas_call(functools.partial(exchange_kernel, n_seq), out_shape=[pltp...  8.85 us
    pallas_call x1, Pallas kernels, per_device(): pl.pallas_call(carried_kernel, out_shape=[pltpu.HBM((rows, width), BF16)]...  1.32 us

profile of v11, /device:TPU:0, one launch (start us, length us, event | category | flops | bytes accessed | tf_op | source)
XLA Modules:
  0.0 10.8 jit_solution(4042877789636156213)
XLA Ops:
  0.6 8.8 %exchange.1 = (bf16[1024,128]{1,0:T(8,128)(2,1)S(1)}, bf16[1024,128]{1,0:T(8,128)(2,1)S(1)}, bf16[1024,128]{1,0:T(8,128)(2,1)S(1)}, bf16[1024,128]{1,0:T(8,128)(...) custom-call(bf16[1024,128]{1,0:T(8,128)(2,1)} %q_hbm.1, ...), custom_call_target="tpu_custom_call" | custom-call | tf_op jit(solution)/shard_map/exchange/pallas_call | solution.py:268
  9.5 1.3 %carried.1 = (bf16[1024,128]{1,0:T(8,128)(2,1)}, bf16[1024,128]{1,0:T(8,128)(2,1)}, bf16[1024,128]{1,0:T(8,128)(2,1)}, bf16[1024,128]{1,0:T(8,128)(2,1)}) custom-call(bf16[1024,128]{1,0:T(8,128)(2,1)S(1)} %get-tuple-element.13.q_ref, bf16[1024,128]{1,0:T(8,128)(2,1)S(1)} %get-tuple-element.14.k_ref, bf16[1024,128]{1,0:T(8,128)(2,1)S(1)} %get-tuple-element.15.v_ref, ...), custom_call_target="tpu_custom_call" | custom-call | tf_op jit(solution)/shard_map/carried/pallas_call | solution.py:291
